TPU v7x, 256 devices: a whole 4x4x8 slice. The times are simulated.
256 devices in a mesh: leaf: 16 (over x, y), blk: 16 (over z, core).
Axes of the slice: x: 4, y: 4, z: 8, core: 2. Of those that a mesh axis runs over, the one named last changes fastest.
Arguments:
- rhs_root: float32 [128, 16384], P(None, ('leaf', 'blk')), may hold values from -6 to 6
- rhs_one: float32 [128, 16384], P(None, ('leaf', 'blk')), may hold values from -6 to 6
- rhs_two: float32 [128, 16384], P(None, ('leaf', 'blk')), may hold values from -6 to 6
- inv_root: bfloat16 [16384, 16384], P(('leaf', 'blk'))
- inv_one: bfloat16 [16384, 8192], P(('leaf', 'blk'))
- inv_two: bfloat16 [16384, 4096], P(('leaf', 'blk'))
- lower_one: bfloat16 [16384, 8192], P(('leaf', 'blk')), may hold values from -0.03125 to 0.03125
- lower_two: bfloat16 [16384, 8192], P(('leaf', 'blk')), may hold values from -0.046875 to 0.046875
- rows_one: int32 [2, 8192], replicated, may hold values from 0 to 16383, as said below
- rows_two: int32 [4, 8192], replicated, may hold values from 0 to 24575, as said below
- count_one: int32 [2], replicated, may hold values from 1 to 8192, 10240 in all
- count_two: int32 [4], replicated, may hold values from 1 to 8192, 20480 in all
Outputs:
- sol_root: float32 [128, 16384], P(None, ('leaf', 'blk'))
- sol_one: float32 [128, 16384], P(None, ('leaf', 'blk'))
- sol_two: float32 [128, 16384], P(None, ('leaf', 'blk'))
Inputs may be any that keep to these rules, and one draw needn't show every extreme that they name: `rows_one`: each list holds 8192 distinct rows of the root, among them the root's first and last row. `rows_two`: each list holds 8192 distinct positions among the root's 16384 rows followed by the parent's 8192 rows, among them the first and the last. `count_one`: the counts sum to 10240. `count_two`: the counts sum to 20480.
All inputs are finite; a program needn't handle non-finite values.
Results may differ from a plain program's by a relative error of at most 0.0041.
Values may be sent and summed in bfloat16 or wider, within the bound.
A program may use at most 128 MiB of HBM per device.

v0:
```python
import jax
import jax.numpy as jnp
from jax import lax
from jax.sharding import PartitionSpec as P


def swapped(array, axis, stride):
    return lax.ppermute(array, axis, [(i, i ^ 1 << stride) for i in range(lax.axis_size(axis))])


def crossing(rhs_full, inverse):
    return lax.dot_general(
        rhs_full, inverse, (((1,), (1,)), ((), ())), preferred_element_type=jnp.float32
    )


def updates(solved, lower, row_lists, row_counts, owner_sep):
    update_terms = jnp.dot(solved.astype(jnp.bfloat16), lower, preferred_element_type=jnp.float32)
    live_mask = jnp.arange(update_terms.shape[1], dtype=jnp.int32) < row_counts[owner_sep]
    update_terms = jnp.where(live_mask[None, :], update_terms, jnp.zeros_like(update_terms))
    listed = lax.dynamic_index_in_dim(row_lists, owner_sep, 0, keepdims=False)
    return (listed, update_terms)


def shards(
    rhs_root,
    rhs_one,
    rhs_two,
    inv_root,
    inv_one,
    inv_two,
    lower_one,
    lower_two,
    rows_one,
    rows_two,
    count_one,
    count_two,
):
    leaves = lax.axis_size("leaf")
    blocks = lax.axis_size("blk")
    leaf_id = lax.axis_index("leaf")
    blk_id = lax.axis_index("blk")
    vectors = rhs_root.shape[0]

    def solve_level(pending, rhs_piece, inverse, level_depth):
        piece_cols = rhs_piece.shape[1]
        group_size = leaves >> level_depth
        owner_sep = leaf_id // group_size
        offset = (leaf_id % group_size * blocks + blk_id) * piece_cols
        local_sum = pending + lax.dynamic_update_slice(
            jnp.zeros_like(pending), rhs_piece, (jnp.int32(0), offset)
        )
        part_sum = lax.psum_scatter(local_sum, "blk", scatter_dimension=1, tiled=True)
        for bit_index in range(group_size.bit_length() - 1):
            part_sum = part_sum + swapped(part_sum, "leaf", bit_index)
        full_rhs = lax.all_gather(part_sum.astype(jnp.bfloat16), "blk", axis=1, tiled=True)
        return (crossing(full_rhs, inverse), owner_sep)

    width_root = inv_root.shape[1]
    width_one = inv_one.shape[1]
    solved_two, owner_two = solve_level(
        jnp.zeros((vectors, inv_two.shape[1]), jnp.float32), rhs_two, inv_two, 2
    )
    listed, update_terms = updates(solved_two, lower_two, rows_two, count_two, owner_two)
    combined = (
        jnp.zeros((vectors, width_root + width_one), jnp.float32).at[:, listed].add(-update_terms)
    )
    solved_one, owner_one = solve_level(combined[:, width_root:], rhs_one, inv_one, 1)
    listed, update_terms = updates(solved_one, lower_one, rows_one, count_one, owner_one)
    root_pending = combined[:, :width_root].at[:, listed].add(-update_terms)
    solved_root, owner_root = solve_level(root_pending, rhs_root, inv_root, 0)
    return (solved_root, solved_one, solved_two)


def solution(mesh):
    return jax.shard_map(
        shards,
        mesh=mesh,
        in_specs=(
            P(None, ("leaf", "blk")),
            P(None, ("leaf", "blk")),
            P(None, ("leaf", "blk")),
            P(("leaf", "blk"), None),
            P(("leaf", "blk"), None),
            P(("leaf", "blk"), None),
            P(("leaf", "blk"), None),
            P(("leaf", "blk"), None),
            P(),
            P(),
            P(),
            P(),
        ),
        out_specs=(P(None, ("leaf", "blk")), P(None, ("leaf", "blk")), P(None, ("leaf", "blk"))),
        check_vma=False,
    )
```

profile of v0, /device:TPU:1, one launch (start us, length us, event | category | flops | bytes accessed | tf_op | source)
XLA Modules:
  0.0 551.6 jit_solution(14083659175169248966)
XLA Ops:
  7.3 1.5 broadcast_in_dim.26
  8.7 1.5 constant_dynamic-update-slice_fusion
  10.3 60.4 %reduce-scatter.4.cloned.1.call-done = f32[128,256]{0,1:T(8,128)} async-done(((f32[128,4096]{0,1:T(8,128)}), f32[128,256]{0,1:T(8,128)}) %reduce-scatter.4.cloned.1.call-update) | async-done | bytes 131088 | tf_op jit(solution)/shard_map/reduce_scatter | solution.py:53
  71.9 2.8 collective-permute-done
  75.7 2.8 collective-permute-start.1
  78.5 4.0 collective-permute-done.1
  85.5 39.2 %all-gather.4.cloned.1.call-done = bf16[128,4096]{0,1:T(8,128)(2,1)} async-done(((bf16[128,256]{0,1:T(8,128)(2,1)}), bf16[128,4096]{0,1:T(8,128)(2,1)}) %all-gather.4.cloned.1.call-update) | async-done | bytes 1048592 | tf_op jit(solution)/shard_map/all_gather | solution.py:56
  124.7 1.7 fusion.8
  126.4 2.7 fusion.3
  129.1 5.6 %copy.17 = f32[8192,128]{1,0:T(8,128)} copy(f32[8192,128]{0,1:T(8,128)} %fusion.3) | data formatting | bytes 8388608 | tf_op jit(solution)/shard_map/neg | solution.py:66
  134.6 49.6 %scatter_custom_fusion = f32[128,24576]{0,1:T(8,128)} fusion(s32[8192]{0:T(1024)S(1)} %bitcast.21, f32[8192,128]{1,0:T(8,128)} %copy.17, f32[]{:T(128)} %constant.70.clone.1), kind=kCustom, calls=%fused_computation.8 | custom fusion | flops 1048576 | bytes 12583424 | tf_op jit(solution)/shard_map/scatter-add | solution.py:66
  184.2 4.4 slice.12
  190.1 58.0 %reduce-scatter.6.cloned.1.call-done = f32[128,512]{0,1:T(8,128)} async-done(((f32[128,8192]{0,1:T(8,128)}), f32[128,512]{0,1:T(8,128)}) %reduce-scatter.6.cloned.1.call-update) | async-done | bytes 262160 | tf_op jit(solution)/shard_map/reduce_scatter | solution.py:53
  249.4 4.2 collective-permute-done.2
  254.6 2.7 collective-permute-start.3
  257.3 5.5 collective-permute-done.3
  264.2 3.9 collective-permute-done.4
  270.4 5.7 %slice.11 = f32[128,16384]{0,1:T(8,128)} slice(f32[128,24576]{0,1:T(8,128)} %scatter_custom_fusion), slice={[0:128], [0:16384]} | slice | bytes 16777216 | tf_op jit(solution)/shard_map/slice | solution.py:70
  276.2 39.0 %all-gather.6.cloned.1.call-done = bf16[128,8192]{0,1:T(8,128)(2,1)} async-done(((bf16[128,512]{0,1:T(8,128)(2,1)}), bf16[128,8192]{0,1:T(8,128)(2,1)}) %all-gather.6.cloned.1.call-update) | async-done | bytes 2097168 | tf_op jit(solution)/shard_map/all_gather | solution.py:56
  315.2 2.1 fusion.9
  317.3 4.0 fusion.1
  321.3 5.6 %copy.18 = f32[8192,128]{1,0:T(8,128)} copy(f32[8192,128]{0,1:T(8,128)} %fusion.1) | data formatting | bytes 8388608 | tf_op jit(solution)/shard_map/neg | solution.py:70
  326.8 46.4 %scatter_fusion = f32[128,16384]{0,1:T(8,128)} fusion(f32[128,16384]{0,1:T(8,128)} %slice.11, s32[8192]{0:T(1024)S(1)} %bitcast.20, f32[8192,128]{1,0:T(8,128)} %copy.18), kind=kCustom, calls=%fused_computation.1 | custom fusion | flops 1048576 | bytes 12615680 | tf_op jit(solution)/shard_map/scatter-add | solution.py:70
  374.7 65.7 %reduce-scatter.8.cloned.1.call-done = f32[128,1024]{0,1:T(8,128)} async-done(((f32[128,16384]{0,1:T(8,128)}), f32[128,1024]{0,1:T(8,128)}) %reduce-scatter.8.cloned.1.call-update) | async-done | bytes 524304 | tf_op jit(solution)/shard_map/reduce_scatter | solution.py:53
  441.5 8.9 %collective-permute-done.5 = f32[128,1024]{0,1:T(8,128)S(1)} collective-permute-done((f32[128,1024]{0,1:T(8,128)}, f32[128,1024]{0,1:T(8,128)S(1)}, u32[]{:S(2)}, u32[]{:S(2)}) %collective-permute-start.5) | collective-permute-done | bytes 524320 | tf_op jit(solution)/shard_map/ppermute | solution.py:8
  451.5 2.8 collective-permute-start.6
  454.3 9.4 %collective-permute-done.6 = f32[128,1024]{0,1:T(8,128)S(1)} collective-permute-done((f32[128,1024]{0,1:T(8,128)S(1)}, f32[128,1024]{0,1:T(8,128)S(1)}, u32[]{:S(2)}, u32[]{:S(2)}) %collective-permute-start.6) | collective-permute-done | bytes 524320 | tf_op jit(solution)/shard_map/ppermute | solution.py:8
  465.0 7.6 %collective-permute-done.7 = f32[128,1024]{0,1:T(8,128)S(1)} collective-permute-done((f32[128,1024]{0,1:T(8,128)S(1)}, f32[128,1024]{0,1:T(8,128)S(1)}, u32[]{:S(2)}, u32[]{:S(2)}) %collective-permute-start.7) | collective-permute-done | bytes 524320 | tf_op jit(solution)/shard_map/ppermute | solution.py:8
  472.7 2.9 collective-permute-start.8
  475.6 11.2 %collective-permute-done.8 = f32[128,1024]{0,1:T(8,128)S(1)} collective-permute-done((f32[128,1024]{0,1:T(8,128)S(1)}, f32[128,1024]{0,1:T(8,128)S(1)}, u32[]{:S(2)}, u32[]{:S(2)}) %collective-permute-start.8) | collective-permute-done | bytes 524320 | tf_op jit(solution)/shard_map/ppermute | solution.py:8
  487.5 53.5 %all-gather.8.cloned.1.call-done = bf16[128,16384]{0,1:T(8,128)(2,1)} async-done(((bf16[128,1024]{0,1:T(8,128)(2,1)}), bf16[128,16384]{0,1:T(8,128)(2,1)}) %all-gather.8.cloned.1.call-update) | async-done | bytes 4194320 | tf_op jit(solution)/shard_map/all_gather | solution.py:56
  541.1 3.7 fusion.10
  (54 shorter events, 18.5 us)
Async XLA Ops:
  7.2 533.9 %copy-start = (bf16[64,16384]{1,0:T(8,128)(2,1)S(1)}, bf16[64,16384]{1,0:T(8,128)(2,1)}, u32[]{:S(2)}) copy-start(bf16[64,16384]{1,0:T(8,128)(2,1)} %param.15) | copy-start | bytes 6291460
  7.2 76.1 %copy-start.8 = (s32[4]{0:T(128)S(1)}, s32[4]{0:T(128)}, u32[]{:S(2)}) copy-start(s32[4]{0:T(128)} %param.23) | copy-start | bytes 52
  7.2 119.2 %copy-start.1 = (bf16[64,8192]{1,0:T(8,128)(2,1)S(1)}, bf16[64,8192]{1,0:T(8,128)(2,1)}, u32[]{:S(2)}) copy-start(bf16[64,8192]{1,0:T(8,128)(2,1)} %param.19) | copy-start | bytes 3145732
  7.2 63.5 %reduce-scatter.4.cloned.1.call-start = ((), (), s32[]{:S(2)}) async-start(), calls=%async_computation.3 | async-start | bytes 2228224 | tf_op jit(solution)/shard_map/reduce_scatter | solution.py:53
  10.3 114.4 %all-gather.4.cloned.1.call-start = ((), (), s32[]{:S(2)}) async-start(), calls=%async_computation.4 | async-start | bytes 1114112 | tf_op jit(solution)/shard_map/all_gather | solution.py:56
  70.7 4.0 collective-permute-start
  75.7 6.8 %collective-permute-start.1 = (f32[128,256]{0,1:T(8,128)S(1)}, f32[128,256]{0,1:T(8,128)S(1)}, u32[]{:S(2)}, u32[]{:S(2)}) collective-permute-start(f32[128,256]{0,1:T(8,128)S(1)} %add.117), channel_id=1, source_target_pairs={{0,32},{16,48},{32,0},{48,16},{64,96},{80,112},{96,64},{112,80},{1... | collective-permute-start | bytes 393224 | tf_op jit(solution)/shard_map/ppermute | solution.py:8
  83.1 165.0 %reduce-scatter.6.cloned.1.call-start = ((), (), s32[]{:S(2)}) async-start(), calls=%async_computation.5 | async-start | bytes 4456448 | tf_op jit(solution)/shard_map/reduce_scatter | solution.py:53
  126.4 8.3 %copy-start.4 = (f32[128,64]{0,1:T(8,128)}, f32[128,64]{0,1:T(8,128)S(1)}, u32[]{:S(2)}) copy-start(f32[128,64]{0,1:T(8,128)S(1)} %fusion.8) | copy-start | bytes 98308
  184.2 4.4 copy-start.5
  188.6 80.4 %copy-start.9 = (s32[2]{0:T(128)S(1)}, s32[2]{0:T(128)}, u32[]{:S(2)}) copy-start(s32[2]{0:T(128)} %param.22) | copy-start | bytes 28
  188.6 81.7 %copy-start.7 = (s32[2,8192]{1,0:T(2,128)S(1)}, s32[2,8192]{1,0:T(2,128)}, u32[]{:S(2)}) copy-start(s32[2,8192]{1,0:T(2,128)} %param.20) | copy-start | bytes 196612
  190.1 125.1 %all-gather.6.cloned.1.call-start = ((), (), s32[]{:S(2)}) async-start(), calls=%async_computation.6 | async-start | bytes 2228224 | tf_op jit(solution)/shard_map/all_gather | solution.py:56
  248.1 5.4 collective-permute-start.2
  254.6 8.2 %collective-permute-start.3 = (f32[128,512]{0,1:T(8,128)S(1)}, f32[128,512]{0,1:T(8,128)S(1)}, u32[]{:S(2)}, u32[]{:S(2)}) collective-permute-start(f32[128,512]{0,1:T(8,128)S(1)} %add.126), channel_id=1, source_target_pairs={{0,32},{16,48},{32,0},{48,16},{64,96},{80,112},{96,64},{112,80},{1... | collective-permute-start | bytes 786440 | tf_op jit(solution)/shard_map/ppermute | solution.py:8
  262.8 5.3 collective-permute-start.4
  268.8 171.5 %reduce-scatter.8.cloned.1.call-start = ((), (), s32[]{:S(2)}) async-start(), calls=%async_computation.7 | async-start | bytes 8912896 | tf_op jit(solution)/shard_map/reduce_scatter | solution.py:53
  270.4 44.8 %copy-start.2 = (bf16[64,8192]{1,0:T(8,128)(2,1)S(1)}, bf16[64,8192]{1,0:T(8,128)(2,1)}, u32[]{:S(2)}) copy-start(bf16[64,8192]{1,0:T(8,128)(2,1)} %param.16) | copy-start | bytes 3145732
  317.3 9.6 %copy-start.3 = (f32[128,64]{0,1:T(8,128)}, f32[128,64]{0,1:T(8,128)S(1)}, u32[]{:S(2)}) copy-start(f32[128,64]{0,1:T(8,128)S(1)} %fusion.9) | copy-start | bytes 98308
  326.8 46.4 %copy-start.6 = (f32[128,64]{0,1:T(8,128)S(1)}, f32[128,64]{0,1:T(8,128)}, u32[]{:S(2)}) copy-start(f32[128,64]{0,1:T(8,128)} %param.12) | copy-start | bytes 98308
  374.6 166.4 %all-gather.8.cloned.1.call-start = ((), (), s32[]{:S(2)}) async-start(), calls=%async_computation.8 | async-start | bytes 4456448 | tf_op jit(solution)/shard_map/all_gather | solution.py:56
  440.3 10.0 %collective-permute-start.5 = (f32[128,1024]{0,1:T(8,128)}, f32[128,1024]{0,1:T(8,128)S(1)}, u32[]{:S(2)}, u32[]{:S(2)}) collective-permute-start(f32[128,1024]{0,1:T(8,128)} %reduce-scatter.8.cloned.1.call-done), channel_id=1, source_target_pairs={{0,16},{16,0},{32,48},{48,32},{64,80},{80,64},{96,112},{112,96},{1... | collective-permute-start | bytes 1572872 | tf_op jit(solution)/shard_map/ppermute | solution.py:8
  451.5 12.2 %collective-permute-start.6 = (f32[128,1024]{0,1:T(8,128)S(1)}, f32[128,1024]{0,1:T(8,128)S(1)}, u32[]{:S(2)}, u32[]{:S(2)}) collective-permute-start(f32[128,1024]{0,1:T(8,128)S(1)} %add.133), channel_id=1, source_target_pairs={{0,32},{16,48},{32,0},{48,16},{64,96},{80,112},{96,64},{112,80},{1... | collective-permute-start | bytes 1572872 | tf_op jit(solution)/shard_map/ppermute | solution.py:8
  463.7 8.9 %collective-permute-start.7 = (f32[128,1024]{0,1:T(8,128)S(1)}, f32[128,1024]{0,1:T(8,128)S(1)}, u32[]{:S(2)}, u32[]{:S(2)}) collective-permute-start(f32[128,1024]{0,1:T(8,128)S(1)} %add.134), channel_id=1, source_target_pairs={{0,64},{16,80},{32,96},{48,112},{64,0},{80,16},{96,32},{112,48},{1... | collective-permute-start | bytes 1572872 | tf_op jit(solution)/shard_map/ppermute | solution.py:8
  472.7 14.0 %collective-permute-start.8 = (f32[128,1024]{0,1:T(8,128)S(1)}, f32[128,1024]{0,1:T(8,128)S(1)}, u32[]{:S(2)}, u32[]{:S(2)}) collective-permute-start(f32[128,1024]{0,1:T(8,128)S(1)} %add.135), channel_id=1, source_target_pairs={{0,128},{16,144},{32,160},{48,176},{64,192},{80,208},{96,224},{112... | collective-permute-start | bytes 1572872 | tf_op jit(solution)/shard_map/ppermute | solution.py:8
Sparse Core Ops, SparseCore 0:
  10.6 60.1 reduce-scatter.3
  83.3 41.3 all-gather.3
  190.2 57.8 reduce-scatter.5
  268.9 46.2 all-gather.5
  374.8 65.5 reduce-scatter.7
  487.7 53.3 all-gather.7
where the time goes:
time: 552 us
  waiting for transfers between devices  373 us (68%)
  other arithmetic  106 us (19%)
  local copies, waits for them, and re-layouts  25.5 us (5%)
  starting transfers between devices  18 us (3%)
  between operations  14.4 us (3%)
  matrix products  14.1 us (3%)
    reduce_scatter x3, waiting for transfers between devices, solve_level(): lax.psum_scatter(local_sum, 'blk', scatter_dimension=1, tiled=True)  184 us
    all_gather x3, waiting for transfers between devices, solve_level(): lax.all_gather(part_sum.astype(jnp.bfloat16), 'blk', axis=1, tiled=True)  132 us
    ppermute x9, waiting for transfers between devices, swapped(): lax.ppermute(array, axis, [(i, i ^ 1 << stride) for i in range(lax.axis_s...  57.4 us
    scatter-add x1, other arithmetic, shards(): jnp.zeros((vectors, width_root + width_one), jnp.float32).at[:, listed]  49.6 us
    scatter-add x1, other arithmetic, shards(): root_pending = combined[:, :width_root].at[:, listed].add(-update_terms)  46.4 us
    ppermute x9, starting transfers between devices, swapped(): lax.ppermute(array, axis, [(i, i ^ 1 << stride) for i in range(lax.axis_s...  17.5 us
  transfers between devices with their start and end apart: 15, of which 15 were waited for; matrix products, arithmetic and copies ran while one was open for 2% of the time, Pallas kernels for 0%

commit v1 on v0

v1 whole, which is shorter than its diff:
```python
import functools

import jax
import jax.numpy as jnp
from jax import lax
from jax.experimental import pallas as pl
from jax.experimental.pallas import tpu as pltpu
from jax.sharding import PartitionSpec as P

VECS = 128
WIDTH = 64
MESH = pl.DeviceIdType.MESH
NX, NY, NZ, NC = 4, 4, 8, 2
ROOT_SLABS = NX * NY
UNROLL = 32


def place_kernel(rows_two, rows_one, live, lower_two, lower_one, out, source, placed):
    length = lower_two.shape[1]
    step = 512

    def turn(i, carry):
        cols = pl.ds(pl.multiple_of(i * step, step), step)
        both = jnp.concatenate([lower_two[:, cols], lower_one[:, cols]], axis=0)
        source[cols, :] = both.astype(jnp.float32).T
        return carry

    lax.fori_loop(0, length // step, turn, 0)

    def clear(i, carry):
        placed[pl.ds(pl.multiple_of(i * step, step), step), :] = jnp.zeros((step, 2 * WIDTH), jnp.float32)
        return carry

    lax.fori_loop(0, placed.shape[0] // step, clear, 0)

    def move(rows, count, lanes):
        def many(i, carry):
            base = pl.multiple_of(i * UNROLL, UNROLL)
            targets = [rows[base + k] for k in range(UNROLL)]
            values = [source[pl.ds(base + k, 1), lanes] for k in range(UNROLL)]
            for k in range(UNROLL):
                placed[pl.ds(targets[k], 1), lanes] = values[k]
            return carry

        def one(j, carry):
            placed[pl.ds(rows[j], 1), lanes] = source[pl.ds(j, 1), lanes]
            return carry

        whole = count // UNROLL
        lax.fori_loop(0, whole, many, 0)
        lax.fori_loop(whole * UNROLL, count, one, 0)

    move(rows_two, live[0], slice(0, WIDTH))
    move(rows_one, live[1], slice(WIDTH, 2 * WIDTH))

    def narrow(i, carry):
        part = placed[pl.ds(pl.multiple_of(i * step, step), step), :].astype(jnp.bfloat16)
        out[pl.ds(i * (step // 128), step // 128)] = part.reshape(step // 128, NC, WIDTH, 2 * WIDTH)
        return carry

    lax.fori_loop(0, placed.shape[0] // step, narrow, 0)


def place(rows_two, rows_one, live, lower_two, lower_one, span):
    smem = pl.BlockSpec(memory_space=pltpu.SMEM)
    vmem = pl.BlockSpec(memory_space=pltpu.VMEM)
    return pl.pallas_call(
        place_kernel,
        out_shape=jax.ShapeDtypeStruct((span // 128, NC, WIDTH, 2 * WIDTH), jnp.bfloat16),
        in_specs=[smem, smem, smem, vmem, vmem],
        out_specs=vmem,
        scratch_shapes=[
            pltpu.VMEM((lower_two.shape[1], 2 * WIDTH), jnp.float32),
            pltpu.VMEM((span, 2 * WIDTH), jnp.float32),
        ],
        compiler_params=pltpu.CompilerParams(vmem_limit_bytes=48 * 2**20),
    )(rows_two, rows_one, live, lower_two, lower_one)


def turned_in(piece):
    padded = jnp.concatenate([piece, jnp.zeros_like(piece)], axis=1)
    return padded.T[:WIDTH]


def turned_out(piece):
    padded = jnp.concatenate([piece, jnp.zeros_like(piece)], axis=0)
    return padded.T[:, :WIDTH]


def main_kernel(
    rhs_root, rhs_one, rhs_two, inv_root_hbm, inv_one_hbm, inv_two_hbm, placed_hbm,
    sol_root, sol_one, sol_two,
    inv_root, inv_one, inv_two, placed,
    full_two, full_one, full_root,
    give_one, take_one, sum_one, ra_one, tb_one, rb_one, vz_one, rz_one,
    give_root, take_root, sum_root, ra_root, tb_root, rb_root, vz_root, rz_root,
    local_sems, z_sems, a_sems, b_sems, s_sems, rs_z_sems, rs_a_sems, rs_b_sems, rs_s_sems,
):
    leaf = lax.axis_index("leaf")
    blk = lax.axis_index("blk")
    x, y = leaf // NY, leaf % NY
    z, c = blk // NC, blk % NC
    half, pair = x // 2, x % 2
    other = 1 - c

    def z_peer(at):
        return (leaf, at * NC + c)

    sibling = (leaf, z * NC + other)

    loads = [
        pltpu.make_async_copy(inv_two_hbm, inv_two, local_sems.at[0]),
        pltpu.make_async_copy(placed_hbm, placed, local_sems.at[1]),
        pltpu.make_async_copy(inv_one_hbm, inv_one, local_sems.at[2]),
        pltpu.make_async_copy(inv_root_hbm, inv_root, local_sems.at[3]),
    ]
    for load in loads:
        load.start()

    barrier = pltpu.get_barrier_semaphore()
    greeted = [z_peer((z + o) % NZ) for o in range(1, NZ)]
    greeted += [(x * NY + (y + o) % NY, blk) for o in range(1, NY)]
    greeted += [((x + o) % NX * NY + y, blk) for o in range(1, NX)]
    greeted += [sibling]
    for device in greeted:
        pl.semaphore_signal(barrier, inc=1, device_id=device, device_id_type=MESH)

    def remote(source, target, sems, index, device):
        return pltpu.make_async_remote_copy(
            src_ref=source,
            dst_ref=target,
            send_sem=sems.at[(0, *index)],
            recv_sem=sems.at[(1, *index)],
            device_id=device,
            device_id_type=MESH,
        )

    def axes_of(core, nx):
        mine_x = pair if nx == 2 else (x if nx == 4 else 0)

        def x_peer(o):
            to = half * 2 + (pair + o) % 2 if nx == 2 else (x + o) % NX
            return (to * NY + y, blk)

        def y_peer(o):
            return (x * NY + (y + o) % NY, blk)

        along_x = (nx, mine_x, x_peer)
        along_y = (NY, y, y_peer)
        if core == 0:
            return along_y, along_x, lambda a, b: b * NY + a
        return along_x, along_y, lambda a, b: a * NY + b

    def by_core(body):
        for core in range(NC):
            pl.when(c == core)(functools.partial(body, core))

    def gather(level, nx, full):
        mine_x = pair if nx == 2 else (x if nx == 4 else 0)
        own = mine_x * NY + y

        def z_copy(o):
            return remote(full.at[own, z, c], full.at[own, z, c], z_sems, (level, o), z_peer((z + o) % NZ))

        def z_arrival(o):
            at = (z + NZ - o) % NZ
            return remote(full.at[own, at, c], full.at[own, at, c], z_sems, (level, o), z_peer(at))

        for o in range(1, NZ):
            z_copy(o).start()
        for o in range(1, NZ):
            z_arrival(o).wait_recv()

        def forward(slab):
            return remote(full.at[slab, :, c], full.at[slab, :, c], s_sems, (level, slab), sibling)

        def planes(core, finish):
            (na, a, a_peer), (nb, b, b_peer), slab_of = axes_of(core, nx)

            def slab_at(oa, ob):
                return slab_of((a + na - oa) % na, (b + nb - ob) % nb)

            def a_copy(oa, slab):
                return remote(full.at[slab, :, c], full.at[slab, :, c], a_sems, (level, oa), a_peer(oa))

            def b_copy(oa, ob, slab):
                return remote(full.at[slab, :, c], full.at[slab, :, c], b_sems, (level, oa, ob), b_peer(ob))

            if finish:
                for oa in range(1, na):
                    a_copy(oa, own).wait_send()
                for oa in range(na):
                    for ob in range(1, nb):
                        b_copy(oa, ob, slab_at(oa, 0)).wait_send()
                return
            for oa in range(1, na):
                a_copy(oa, own).start()
            for ob in range(1, nb):
                b_copy(0, ob, own).start()
            forward(own).start()
            for oa in range(1, na):
                slab = slab_at(oa, 0)
                a_copy(oa, slab).wait_recv()
                for ob in range(1, nb):
                    b_copy(oa, ob, slab).start()
                forward(slab).start()
            for oa in range(na):
                for ob in range(1, nb):
                    slab = slab_at(oa, ob)
                    b_copy(oa, ob, slab).wait_recv()
                    forward(slab).start()

        by_core(lambda core: planes(core, False))

        def finish():
            for o in range(1, NZ):
                z_copy(o).wait_send()
            by_core(lambda core: planes(core, True))
            for slab in range(nx * NY):
                forward(slab).wait_send()

        def arrived(slab):
            remote(full.at[slab, :, other], full.at[slab, :, other], s_sems, (level, slab), sibling).wait_recv()

        return arrived, finish

    def solve(nx, full, inverse, arrived):
        total = jnp.zeros((WIDTH, VECS), jnp.float32)
        wide = NZ * NC * WIDTH
        for slab in range(nx * NY):
            arrived(slab)
            total += jnp.dot(
                inverse[:, slab * wide:(slab + 1) * wide],
                full[slab].reshape(wide, VECS),
                preferred_element_type=jnp.float32,
            )
        return total

    def reduce(level, nx, first, solved, give, take, sums, ra, tb, rb, vz, rz):
        def terms(slab, parity):
            lower = placed[pl.ds((first + slab) * NZ, NZ), parity]
            return jnp.dot(
                lower.reshape(NZ * WIDTH, 2 * WIDTH), solved, preferred_element_type=jnp.float32
            ).reshape(NZ, WIDTH, VECS)

        def pass_on(slab):
            return remote(give.at[slab], take.at[slab], rs_s_sems, (level, slab), sibling)

        def planes(core, finish):
            (na, a, a_peer), (nb, b, b_peer), slab_of = axes_of(core, nx)
            (ma, a2, _), (mb, b2, _), slab_of2 = axes_of(1 - core, nx)

            def a_copy(oa, ob):
                slab = slab_of((a + oa) % na, (b + ob) % nb)
                return remote(sums.at[slab], ra.at[oa - 1, ob], rs_a_sems, (level, oa, ob), a_peer(oa))

            def b_copy(ob):
                return remote(tb.at[ob], rb.at[ob - 1], rs_b_sems, (level, ob), b_peer(ob))

            if finish:
                for ob in range(nb):
                    for oa in range(1, na):
                        a_copy(oa, ob).wait_send()
                for ob in range(1, nb):
                    b_copy(ob).wait_send()
                return
            for ob in [*range(1, mb), 0]:
                for oa in [*range(1, ma), 0]:
                    slab = slab_of2((a2 + oa) % ma, (b2 + ob) % mb)
                    give[slab] = terms(slab, other).astype(jnp.bfloat16)
                    pass_on(slab).start()
            for ob in [*range(1, nb), 0]:
                for oa in [*range(1, na), 0]:
                    slab = slab_of((a + oa) % na, (b + ob) % nb)
                    part = terms(slab, c)
                    pass_on(slab).wait_recv()
                    sums[slab] = (part + take[slab].astype(jnp.float32)).astype(jnp.bfloat16)
                    if oa:
                        a_copy(oa, ob).start()
            for ob in [*range(1, nb), 0]:
                total = sums[slab_of(a, (b + ob) % nb)].astype(jnp.float32)
                for oa in range(1, na):
                    a_copy(oa, ob).wait_recv()
                    total += ra[oa - 1, ob].astype(jnp.float32)
                if ob:
                    tb[ob] = total.astype(jnp.bfloat16)
                    b_copy(ob).start()
                else:
                    for ob2 in range(1, nb):
                        b_copy(ob2).wait_recv()
                        total += rb[ob2 - 1].astype(jnp.float32)
                    vz[...] = total.astype(jnp.bfloat16)

        by_core(lambda core: planes(core, False))

        def z_copy(o):
            return remote(vz.at[(z + o) % NZ], rz.at[o - 1], rs_z_sems, (level, o), z_peer((z + o) % NZ))

        for o in range(1, NZ):
            z_copy(o).start()
        total = vz[z].astype(jnp.float32)
        for o in range(1, NZ):
            z_copy(o).wait_recv()
            total += rz[o - 1].astype(jnp.float32)

        def finish():
            for o in range(1, NZ):
                z_copy(o).wait_send()
            by_core(lambda core: planes(core, True))
            for slab in range(nx * NY):
                pass_on(slab).wait_send()

        return total, finish

    finishes = []

    full_two[y, z, c] = turned_in(rhs_two[...]).astype(jnp.bfloat16)
    pl.semaphore_wait(barrier, len(greeted))
    arrived, finish = gather(0, 1, full_two)
    finishes.append(finish)
    loads[0].wait()
    solved_two = solve(1, full_two, inv_two, arrived)
    sol_two[...] = turned_out(solved_two)
    y_two = solved_two.astype(jnp.bfloat16)

    loads[1].wait()
    stacked = jnp.concatenate([y_two, jnp.zeros_like(y_two)], axis=0)
    moved, finish = reduce(
        0, 2, ROOT_SLABS, stacked, give_one, take_one, sum_one, ra_one, tb_one, rb_one, vz_one, rz_one
    )
    finishes.append(finish)
    full_one[pair * NY + y, z, c] = (turned_in(rhs_one[...]) - moved).astype(jnp.bfloat16)
    arrived, finish = gather(1, 2, full_one)
    finishes.append(finish)
    loads[2].wait()
    solved_one = solve(2, full_one, inv_one, arrived)
    sol_one[...] = turned_out(solved_one)
    y_one = solved_one.astype(jnp.bfloat16)

    stacked = jnp.concatenate([y_two, y_one], axis=0)
    moved, finish = reduce(
        1, 4, 0, stacked, give_root, take_root, sum_root, ra_root, tb_root, rb_root, vz_root, rz_root
    )
    finishes.append(finish)
    full_root[x * NY + y, z, c] = (turned_in(rhs_root[...]) - moved).astype(jnp.bfloat16)
    arrived, finish = gather(2, 4, full_root)
    finishes.append(finish)
    loads[3].wait()
    sol_root[...] = turned_out(solve(4, full_root, inv_root, arrived))

    for finish in finishes:
        finish()


def substitute(rhs_root, rhs_one, rhs_two, inv_root, inv_one, inv_two, placed):
    vmem = pl.BlockSpec(memory_space=pltpu.VMEM)
    hbm = pl.BlockSpec(memory_space=pl.ANY)
    bf16 = jnp.bfloat16

    def slabs(*lead):
        return pltpu.VMEM((*lead, NZ, WIDTH, VECS), bf16)

    def level(nx):
        return [
            slabs(nx * NY), slabs(nx * NY), slabs(nx * NY),
            slabs(3, NY), slabs(NY), slabs(3),
            slabs(), pltpu.VMEM((NZ - 1, WIDTH, VECS), bf16),
        ]

    sems = pltpu.SemaphoreType.DMA
    out = jax.ShapeDtypeStruct((VECS, WIDTH), jnp.float32)
    return pl.pallas_call(
        main_kernel,
        out_shape=(out, out, out),
        in_specs=[vmem] * 3 + [hbm] * 4,
        out_specs=(vmem,) * 3,
        scratch_shapes=[
            pltpu.VMEM(inv_root.shape, bf16),
            pltpu.VMEM(inv_one.shape, bf16),
            pltpu.VMEM(inv_two.shape, bf16),
            pltpu.VMEM(placed.shape, bf16),
            pltpu.VMEM((NY, NZ, NC, WIDTH, VECS), bf16),
            pltpu.VMEM((2 * NY, NZ, NC, WIDTH, VECS), bf16),
            pltpu.VMEM((NX * NY, NZ, NC, WIDTH, VECS), bf16),
            *level(2),
            *level(4),
            sems((4,)),
            sems((2, 3, NZ)),
            sems((2, 3, 4)),
            sems((2, 3, 4, 4)),
            sems((2, 3, NX * NY)),
            sems((2, 2, NZ)),
            sems((2, 2, 4, 4)),
            sems((2, 2, 4)),
            sems((2, 2, NX * NY)),
        ],
        compiler_params=pltpu.CompilerParams(
            collective_id=0, has_side_effects=True, vmem_limit_bytes=56 * 2**20
        ),
    )(rhs_root, rhs_one, rhs_two, inv_root, inv_one, inv_two, placed)


def shards(
    rhs_root,
    rhs_one,
    rhs_two,
    inv_root,
    inv_one,
    inv_two,
    lower_one,
    lower_two,
    rows_one,
    rows_two,
    count_one,
    count_two,
):
    leaf = lax.axis_index("leaf")
    sep_two = leaf // NY
    sep_one = leaf // (2 * NY)

    def own(array, sep):
        return lax.dynamic_index_in_dim(array, sep, 0, keepdims=False)

    live = jnp.stack([own(count_two, sep_two), own(count_one, sep_one)])
    placed = place(
        own(rows_two, sep_two), own(rows_one, sep_one), live, lower_two, lower_one,
        inv_root.shape[1] + inv_one.shape[1],
    )
    return substitute(rhs_root, rhs_one, rhs_two, inv_root, inv_one, inv_two, placed)


def solution(mesh):
    cut = P(None, ("leaf", "blk"))
    rows = P(("leaf", "blk"), None)
    return jax.shard_map(
        shards,
        mesh=mesh,
        in_specs=(cut, cut, cut, rows, rows, rows, rows, rows, P(), P(), P(), P()),
        out_specs=(cut, cut, cut),
        check_vma=False,
    )
```

time: 552 us -> 164 us (0.30)
  waiting for transfers between devices: 373 us -> 0 us
  Pallas kernels: 0 us -> 147 us
  other arithmetic: 106 us -> 1.37 us
  starting transfers between devices: 18 us -> 0 us
  matrix products: 14.1 us -> 0 us
  between operations: 14.4 us -> 0.7 us
  local copies, waits for them, and re-layouts: 25.5 us -> 14.9 us
    reduce_scatter x3 -> x0, waiting for transfers between devices: 184 us -> none  [solve_level(): lax.psum_scatter(local_sum, 'blk', scatter_dimension=1, tiled=True)]
    pallas_call x0 -> x2, Pallas kernels: none -> 147 us  [the longest x1 131 us: substitute(): pl.pallas_call(main_kernel, out_shape=(out, out, out), in_specs=[vmem] *...]
    all_gather x3 -> x0, waiting for transfers between devices: 132 us -> none  [solve_level(): lax.all_gather(part_sum.astype(jnp.bfloat16), 'blk', axis=1, tiled=True)]
    scatter-add x2 -> x0, other arithmetic: 96 us -> none  [the longest x1 49.6 us: shards(): jnp.zeros((vectors, width_root + width_one), jnp.float32).at[:, listed]]
    ppermute x9 -> x0, waiting for transfers between devices: 57.4 us -> none  [swapped(): lax.ppermute(array, axis, [(i, i ^ 1 << stride) for i in range(lax.axis_s...]
    ppermute x9 -> x0, starting transfers between devices: 17.5 us -> none  [swapped(): lax.ppermute(array, axis, [(i, i ^ 1 << stride) for i in range(lax.axis_s...]
    dot_general x5 -> x0, matrix products: 14.1 us -> none  [the longest x3 7.45 us: crossing(): lax.dot_general(rhs_full, inverse, (((1,), (1,)), ((), ())), preferred_el...]
    neg x2 -> x0, local copies, waits for them, and re-layouts: 11.1 us -> none  [the longest x1 5.57 us: shards(): root_pending = combined[:, :width_root].at[:, listed].add(-update_terms)]
  transfers between devices with their start and end apart: 15 -> 0, of which waited for: 15 -> 0; matrix products, arithmetic and copies ran while one was open for 2% -> 0% of each run, Pallas kernels for 0% -> 0%
where the time goes in v1:
time: 164 us; the launch traced here: 163 us
  Pallas kernels  147 us (90%)
  local copies, waits for them, and re-layouts  14.9 us (9%)
    pallas_call x1, Pallas kernels, substitute(): pl.pallas_call(main_kernel, out_shape=(out, out, out), in_specs=[vmem] *...  131 us
    pallas_call x1, Pallas kernels, place(): pl.pallas_call(place_kernel, out_shape=jax.ShapeDtypeStruct((span // 128,...  16 us
    unnamed x9, local copies, waits for them, and re-layouts  6.88 us
    pallas_call x3, local copies, waits for them, and re-layouts, substitute(): pl.pallas_call(main_kernel, out_shape=(out, out, out), in_specs=[vmem] *...  4.61 us
    dynamic_slice x4, local copies, waits for them, and re-layouts, own(): return lax.dynamic_index_in_dim(array, sep, 0, keepdims=False)  3.41 us

profile of v1, /device:TPU:1, one launch (start us, length us, event | category | flops | bytes accessed | tf_op | source)
XLA Modules:
  0.0 163.5 jit_solution(5801028620801085905)
XLA Ops:
  0.6 0.0 copy-start
  0.7 1.3 dynamic_slice.18
  1.9 1.2 dynamic_slice.19
  3.2 1.4 pad_add_fusion.live
  4.6 0.9 constant_dynamic-slice_fusion
  5.4 0.0 copy-done
  5.5 1.5 copy.15.rhs_root
  7.0 1.5 copy.16.rhs_one
  8.4 1.5 copy.17.rhs_two
  9.9 0.0 copy-start.1
  9.9 1.2 copy-done.1
  11.1 0.0 copy-start.2
  11.1 1.2 copy-done.2
  12.3 16.0 %shard_map.139.placed_hbm = bf16[192,2,64,128]{3,2,1,0:T(8,128)(2,1)} custom-call(s32[8192]{0:T(1024)S(1)} %bitcast.3, s32[8192]{0:T(1024)S(1)} %bitcast.2, s32[2]{0:T(128)S(1)} %pad_add_fusion.live, bf16[64,8192]{1,0:T(8,128)(2,1)S(1)} %copy-done.1, bf16[64,8192]{1,0:T(8,128)(2,1)S(1)} %copy-done.2), custom_call_target="tpu_custom_call" | custom-call | tf_op jit(solution)/shard_map/pallas_call | solution.py:67
  28.3 130.5 %shard_map.140 = (f32[128,64]{1,0:T(8,128)}, f32[128,64]{1,0:T(8,128)}, f32[128,64]{1,0:T(8,128)}) custom-call(f32[128,64]{1,0:T(8,128)} %copy.15.rhs_root, f32[128,64]{1,0:T(8,128)} %copy.16.rhs_one, f32[128,64]{1,0:T(8,128)} %copy.17.rhs_two, bf16[64,16384]{1,0:T(8,128)(2,1)} %inv_root_hbm.1, bf16[64,8192]{1,0:T(8,128)(2,1)} %inv_one_hbm.1, ...), custom_call_target="tpu_custom_call" | custom-call | tf_op jit(solution)/shard_map/pallas_call | solution.py:372
  158.9 1.5 copy.18
  160.4 1.5 copy.19
  162.0 1.5 copy.20
  (1 shorter events, 0.0 us)
Async XLA Ops:
  0.6 4.8 %copy-start = (s32[4,8192]{1,0:T(4,128)S(1)}, s32[4,8192]{1,0:T(4,128)}, u32[]{:S(2)}) copy-start(s32[4,8192]{1,0:T(4,128)} %param.21) | copy-start | bytes 393220
  9.9 1.2 copy-start.1
  11.1 1.2 copy-start.2

commit v2 on v0

v2 whole, which is shorter than its diff:
```python
import functools

import jax
import jax.numpy as jnp
from jax import lax
from jax.experimental import pallas as pl
from jax.experimental.pallas import tpu as pltpu
from jax.sharding import PartitionSpec as P

VECS = 128
WIDTH = 64
MESH = pl.DeviceIdType.MESH
NX, NY, NZ, NC = 4, 4, 8, 2
ROOT_SLABS = NX * NY
UNROLL = 32
PARTS = 2


def place_kernel(
    rows_two_hbm, rows_one_hbm, count_two, count_one, lower_two_hbm, lower_one_hbm, out_hbm,
    rows_two, rows_one, lower_two, lower_one, source, placed, out, in_sems, out_sems,
):
    leaf = lax.axis_index("leaf")
    sep_two, sep_one = leaf // NY, leaf // (2 * NY)
    loads = [
        pltpu.make_async_copy(lower_two_hbm, lower_two, in_sems.at[0]),
        pltpu.make_async_copy(lower_one_hbm, lower_one, in_sems.at[1]),
        pltpu.make_async_copy(rows_two_hbm.at[sep_two], rows_two, in_sems.at[2]),
        pltpu.make_async_copy(rows_one_hbm.at[sep_one], rows_one, in_sems.at[3]),
    ]
    for load in loads:
        load.start()
    length = lower_two.shape[1]
    step = 512

    def clear(i, carry):
        placed[pl.ds(pl.multiple_of(i * step, step), step), :] = jnp.zeros((step, 2 * WIDTH), jnp.float32)
        return carry

    lax.fori_loop(0, placed.shape[0] // step, clear, 0)
    for load in loads:
        load.wait()

    def turn(i, carry):
        cols = pl.ds(pl.multiple_of(i * step, step), step)
        both = jnp.concatenate([lower_two[:, cols], lower_one[:, cols]], axis=0)
        source[cols, :] = both.astype(jnp.float32).T
        return carry

    lax.fori_loop(0, length // step, turn, 0)

    def move(rows, count, lanes):
        def many(i, carry):
            base = pl.multiple_of(i * UNROLL, UNROLL)
            targets = [rows[base + k] for k in range(UNROLL)]
            values = [source[pl.ds(base + k, 1), lanes] for k in range(UNROLL)]
            for k in range(UNROLL):
                placed[pl.ds(targets[k], 1), lanes] = values[k]
            return carry

        def one(j, carry):
            placed[pl.ds(rows[j], 1), lanes] = source[pl.ds(j, 1), lanes]
            return carry

        whole = count // UNROLL
        lax.fori_loop(0, whole, many, 0)
        lax.fori_loop(whole * UNROLL, count, one, 0)

    move(rows_two, count_two[sep_two], slice(0, WIDTH))
    move(rows_one, count_one[sep_one], slice(WIDTH, 2 * WIDTH))

    chunks = out_sems.shape[0]
    tall = placed.shape[0] // chunks
    stores = []
    for chunk in range(chunks):
        def narrow(i, carry):
            part = placed[pl.ds(pl.multiple_of(i * step, step), step), :].astype(jnp.bfloat16)
            out[pl.ds(i * (step // 128), step // 128)] = part.reshape(step // 128, NC, WIDTH, 2 * WIDTH)
            return carry

        lax.fori_loop(chunk * tall // step, (chunk + 1) * tall // step, narrow, 0)
        piece = slice(chunk * tall // 128, (chunk + 1) * tall // 128)
        stores.append(pltpu.make_async_copy(out.at[piece], out_hbm.at[piece], out_sems.at[chunk]))
        stores[-1].start()
    for store in stores:
        store.wait()


def place(rows_two, rows_one, count_two, count_one, lower_two, lower_one, span):
    smem = pl.BlockSpec(memory_space=pltpu.SMEM)
    hbm = pl.BlockSpec(memory_space=pl.ANY)
    length = lower_two.shape[1]
    result = (span // 128, NC, WIDTH, 2 * WIDTH)
    return pl.pallas_call(
        place_kernel,
        out_shape=jax.ShapeDtypeStruct(result, jnp.bfloat16),
        in_specs=[hbm, hbm, smem, smem, hbm, hbm],
        out_specs=hbm,
        scratch_shapes=[
            pltpu.SMEM((length,), jnp.int32),
            pltpu.SMEM((length,), jnp.int32),
            pltpu.VMEM(lower_two.shape, jnp.bfloat16),
            pltpu.VMEM(lower_one.shape, jnp.bfloat16),
            pltpu.VMEM((length, 2 * WIDTH), jnp.float32),
            pltpu.VMEM((span, 2 * WIDTH), jnp.float32),
            pltpu.VMEM(result, jnp.bfloat16),
            pltpu.SemaphoreType.DMA((4,)),
            pltpu.SemaphoreType.DMA((4,)),
        ],
        compiler_params=pltpu.CompilerParams(vmem_limit_bytes=60 * 2**20),
    )(rows_two, rows_one, count_two, count_one, lower_two, lower_one)


def ring_order(size):
    return {1: (0,), 2: (1, 0), 4: (2, 1, 3, 0)}[size]


def main_kernel(
    rhs_root, rhs_one, rhs_two, inv_root_hbm, inv_one_hbm, inv_two_hbm, placed_hbm,
    sol_root, sol_one, sol_two,
    inv_root, inv_one, inv_two, placed,
    full_two, full_one, full_root,
    *rest,
):
    level_refs = {"one": rest[:11], "root": rest[11:22]}
    local_sems, z_sems, a_sems, b_sems, s_sems, rz_sems, ra_sems, rb_sems, rs_sems = rest[22:]
    leaf = lax.axis_index("leaf")
    blk = lax.axis_index("blk")
    x, y = leaf // NY, leaf % NY
    z, c = blk // NC, blk % NC
    half, pair = x // 2, x % 2
    other = 1 - c
    low, high = slice(0, NZ // 2), slice(NZ // 2, NZ)

    def z_peer(at):
        return (leaf, at * NC + c)

    sibling = (leaf, z * NC + other)

    loads = [
        pltpu.make_async_copy(inv_two_hbm, inv_two, local_sems.at[0]),
        pltpu.make_async_copy(placed_hbm, placed, local_sems.at[1]),
        pltpu.make_async_copy(inv_one_hbm, inv_one, local_sems.at[2]),
        pltpu.make_async_copy(inv_root_hbm, inv_root, local_sems.at[3]),
    ]
    for load in loads:
        load.start()

    barrier = pltpu.get_barrier_semaphore()
    greeted = [z_peer((z + o) % NZ) for o in range(1, NZ)]
    greeted += [(x * NY + (y + o) % NY, blk) for o in (1, 3)]
    greeted += [((x + o) % NX * NY + y, blk) for o in (1, 3)]
    greeted += [sibling]
    for device in greeted:
        pl.semaphore_signal(barrier, inc=1, device_id=device, device_id_type=MESH)

    def remote(source, target, sems, index, device):
        return pltpu.make_async_remote_copy(
            src_ref=source,
            dst_ref=target,
            send_sem=sems.at[(0, *index)],
            recv_sem=sems.at[(1, *index)],
            device_id=device,
            device_id_type=MESH,
        )

    def part_of(h):
        return slice(h * WIDTH // PARTS, (h + 1) * WIDTH // PARTS)

    def axes_of(core, nx):
        mine_x = {1: 0, 2: pair, 4: x}[nx]

        def x_peer(o):
            to = half * 2 + (pair + o) % 2 if nx == 2 else (x + o) % NX
            return (to * NY + y, blk)

        def y_peer(o):
            return (x * NY + (y + o) % NY, blk)

        along_x = (nx, mine_x, x_peer)
        along_y = (NY, y, y_peer)
        first, second = (along_y, along_x) if core == 0 else (along_x, along_y)

        def slab(oa, ob):
            at_a, at_b = (first[1] + oa) % first[0], (second[1] + ob) % second[0]
            return at_b * NY + at_a if core == 0 else at_a * NY + at_b

        return first, second, slab

    def by_core(body):
        for core in range(NC):
            pl.when(c == core)(functools.partial(body, core))

    def gather_steps(core, level, nx, full, sent):
        (na, _, a_peer), (nb, _, b_peer), slab_at = axes_of(core, nx)

        def start(make):
            make().start()
            sent.append(make)

        def steps(h):
            rows = part_of(h)
            own = slab_at(0, 0)

            def piece(at):
                return full.at[own, at, c, rows]

            def z_copy(o):
                return remote(piece(z), piece(z), z_sems, (level, h, o), z_peer((z + o) % NZ))

            def z_arrival(o):
                at = (z + NZ - o) % NZ
                return remote(piece(at), piece(at), z_sems, (level, h, o), z_peer(at))

            def plane(slab, zs, parity=c):
                return full.at[slab, zs, parity, rows]

            def forward(slab):
                start(lambda: remote(plane(slab, slice(None)), plane(slab, slice(None)), s_sems, (level, h, slab), sibling))

            def a_copy(kind, slab):
                zs = (slice(None), slice(None), low, high)[kind]
                return remote(plane(slab, zs), plane(slab, zs), a_sems, (level, h, kind), a_peer((1, -1, 1, -1)[kind] % na))

            def b_copy(oa, kind, slab):
                zs = (slice(None), slice(None), low, high)[kind]
                return remote(
                    plane(slab, zs), plane(slab, zs), b_sems, (level, h, oa, kind), b_peer((1, -1, 1, -1)[kind] % nb)
                )

            def a_send(kind, slab):
                start(lambda: a_copy(kind, slab))

            def b_send(oa, kind, slab):
                start(lambda: b_copy(oa, kind, slab))

            def b_first(oa):
                if nb > 1:
                    b_send(oa, 0, slab_at(oa, 0))
                if nb > 2:
                    b_send(oa, 1, slab_at(oa, 0))

            def step_z():
                for o in range(1, NZ):
                    start(functools.partial(z_copy, o))

            def step_own():
                for o in range(1, NZ):
                    z_arrival(o).wait_recv()
                if na > 1:
                    a_send(0, own)
                if na > 2:
                    a_send(1, own)
                b_first(0)
                forward(own)

            def step_a_near():
                for kind, oa in ((0, na - 1), (1, 1))[: {1: 0, 2: 1, 4: 2}[na]]:
                    slab = slab_at(oa, 0)
                    a_copy(kind, slab).wait_recv()
                    if na > 2:
                        a_send(kind + 2, slab)
                    b_first(oa)
                    forward(slab)

            def step_a_far():
                if na > 2:
                    slab = slab_at(2, 0)
                    a_copy(2, slab).wait_recv()
                    a_copy(3, slab).wait_recv()
                    b_first(2)
                    forward(slab)

            a_order = {1: (0,), 2: (0, 1), 4: (0, 3, 1, 2)}[na]

            def step_b_near():
                for oa in a_order:
                    for kind, ob in ((0, nb - 1), (1, 1))[: {1: 0, 2: 1, 4: 2}[nb]]:
                        slab = slab_at(oa, ob)
                        b_copy(oa, kind, slab).wait_recv()
                        if nb > 2:
                            b_send(oa, kind + 2, slab)
                        forward(slab)

            def step_b_far():
                if nb > 2:
                    for oa in a_order:
                        slab = slab_at(oa, 2)
                        b_copy(oa, 2, slab).wait_recv()
                        b_copy(oa, 3, slab).wait_recv()
                        forward(slab)

            return [step_z, step_own, step_a_near, step_a_far, step_b_near, step_b_far]

        return steps

    def solve(core, level, nx, full, inverse, out):
        (na, _, _), (nb, _, _), slab_at = axes_of(core, nx)
        wide = NZ * NC * WIDTH
        total = jnp.zeros((WIDTH, VECS), jnp.float32)
        for ob in range(nb):
            for oa in range(na):
                slab = slab_at(oa, ob)
                for h in range(PARTS):
                    block = full.at[slab, :, other, part_of(h)]
                    remote(block, block, s_sems, (level, h, slab), sibling).wait_recv()
                total += jnp.dot(
                    inverse[:, pl.ds(pl.multiple_of(slab * wide, wide), wide)],
                    full[slab].reshape(wide, VECS),
                    preferred_element_type=jnp.float32,
                )
        out[...] = total

    def reduce_steps(core, level, nx, first, solved, refs, sent):
        give, take, sums, low_a, high_a, near_a, totals, half_b, near_b, whole, landed = refs
        (na, _, a_peer), (nb, _, b_peer), slab_at = axes_of(core, nx)
        (ma, _, _), (mb, _, _), slab_there = axes_of(1 - core, nx)

        def start(make):
            make().start()
            sent.append(make)

        def terms(slab, parity, rows):
            lower = placed[pl.ds((first + slab) * NZ, NZ), parity, rows]
            return jnp.dot(
                lower.reshape(NZ * WIDTH // PARTS, 2 * WIDTH), solved, preferred_element_type=jnp.float32
            ).reshape(NZ, WIDTH // PARTS, VECS)

        def pass_on(slab, h):
            rows = part_of(h)
            return remote(give.at[slab, :, rows], take.at[slab, :, rows], rs_sems, (level, h, slab), sibling)

        def wide(ref, index):
            return ref[index].astype(jnp.float32)

        def local(slab, h):
            part = terms(slab, c, part_of(h))
            pass_on(slab, h).wait_recv()
            return part + wide(take, (slab, slice(None), part_of(h)))

        def give_all(h):
            for ob in ring_order(mb):
                for oa in ring_order(ma):
                    slab = slab_there(oa, ob)
                    give[slab, :, part_of(h)] = terms(slab, other, part_of(h)).astype(jnp.bfloat16)
                    start(functools.partial(pass_on, slab, h))

        def a_copy(kind, ob, h):
            rows = part_of(h)
            slab = slab_at((2, 2, 1, -1)[kind] % na, ob)
            zs = (low, high, slice(None), slice(None))[kind]
            target = (low_a.at[ob, :, rows], high_a.at[ob, :, rows], near_a.at[0, ob, :, rows], near_a.at[1, ob, :, rows])
            return remote(
                sums.at[slab, zs, rows], target[kind], ra_sems, (level, h, ob, kind), a_peer((1, -1, 1, -1)[kind] % na)
            )

        def b_copy(kind, h):
            rows = part_of(h)
            zs = (low, high, slice(None), slice(None))[kind]
            target = (half_b.at[0, :, rows], half_b.at[1, :, rows], near_b.at[0, :, rows], near_b.at[1, :, rows])
            return remote(
                totals.at[(2, 2, 1, -1)[kind] % nb, zs, rows], target[kind], rb_sems, (level, h, kind),
                b_peer((1, -1, 1, -1)[kind] % nb),
            )

        def joined(value, extra, at_low):
            lower, upper = value[: NZ // 2], value[NZ // 2 :]
            lower, upper = (lower + extra, upper) if at_low else (lower, upper + extra)
            return jnp.concatenate([lower, upper], axis=0)

        def far(h, ob):
            if na > 2:
                sums[slab_at(2, ob), :, part_of(h)] = local(slab_at(2, ob), h).astype(jnp.bfloat16)
                start(lambda: a_copy(0, ob, h))
                start(lambda: a_copy(1, ob, h))

        def near(h, ob):
            rows = part_of(h)
            for kind, oa in ((2, 1), (3, na - 1))[: {1: 0, 2: 1, 4: 2}[na]]:
                value = local(slab_at(oa, ob), h)
                if na > 2:
                    a_copy(kind - 2, ob, h).wait_recv()
                    value = joined(value, wide((low_a, high_a)[kind - 2], (ob, slice(None), rows)), kind == 2)
                sums[slab_at(oa, ob), :, rows] = value.astype(jnp.bfloat16)
                start(functools.partial(a_copy, kind, ob, h))

        def close(h, ob):
            rows = part_of(h)
            value = local(slab_at(0, ob), h)
            for side in range({1: 0, 2: 1, 4: 2}[na]):
                a_copy(2 + side, ob, h).wait_recv()
                value += wide(near_a, (side, ob, slice(None), rows))
            if ob == 0:
                for side in range({1: 0, 2: 1, 4: 2}[nb]):
                    b_copy(2 + side, h).wait_recv()
                    value += wide(near_b, (side, slice(None), rows))
                whole[:, rows] = value
                totals[0, :, rows] = value.astype(jnp.bfloat16)
                for o in range(1, NZ):
                    start(functools.partial(z_copy, o, h))
                return
            if nb > 2 and ob != 2:
                kind = 0 if ob == 1 else 1
                b_copy(kind, h).wait_recv()
                value = joined(value, wide(half_b, (kind, slice(None), rows)), kind == 0)
            totals[ob, :, rows] = value.astype(jnp.bfloat16)
            if nb > 2 and ob == 2:
                start(lambda: b_copy(0, h))
                start(lambda: b_copy(1, h))
            else:
                start(lambda: b_copy(2 if ob == 1 else 3, h))

        def z_copy(o, h):
            rows = part_of(h)
            return remote(
                totals.at[0, (z + o) % NZ, rows], landed.at[o - 1, rows], rz_sems, (level, h, o), z_peer((z + o) % NZ)
            )

        def result(h):
            rows = part_of(h)
            value = whole[z, rows]
            for o in range(1, NZ):
                z_copy(o, h).wait_recv()
                value += wide(landed, (o - 1, rows))
            return value

        return give_all, far, near, close, result, ring_order(nb)

    def step_down(core, level, nx, first, solved, refs, rhs, full, inverse, out):
        sent = []
        give_all, far, near, close, result, order = reduce_steps(core, level, nx, first, solved, refs, sent)
        spread = gather_steps(core, level + 1, nx, full, sent)
        slab = axes_of(core, nx)[2](0, 0)

        def tail(h):
            steps = spread(h)

            def update():
                rows = part_of(h)
                full[slab, z, c, rows] = (rhs[rows] - result(h)).astype(jnp.bfloat16)
                steps[0]()

            return [update, *steps[1:]]

        work = [(h, ob) for h in range(PARTS) for ob in order]
        tails = [tail(h) for h in range(PARTS)]
        for t in range(len(work) + 2):
            if t < len(work):
                h, ob = work[t]
                if ob == order[0]:
                    give_all(h)
                far(h, ob)
            if 1 <= t <= len(work):
                near(*work[t - 1])
            if t >= 2:
                close(*work[t - 2])
            for h in range(PARTS - 1):
                if t > (h + 1) * len(order) + 1 and tails[h]:
                    tails[h].pop(0)()
        while any(tails):
            for steps in tails[::-1]:
                if steps:
                    steps.pop(0)()
        solve(core, level + 1, nx, full, inverse, out)
        for make in sent:
            make().wait_send()

    full_two[y, z, c] = rhs_two[...].astype(jnp.bfloat16)
    pl.semaphore_wait(barrier, len(greeted))

    def top(core):
        sent = []
        spread = gather_steps(core, 0, 1, full_two, sent)
        for step in zip(*[spread(h) for h in range(PARTS)]):
            for part in step:
                part()
        loads[0].wait()
        solve(core, 0, 1, full_two, inv_two, sol_two)
        for make in sent:
            make().wait_send()

    by_core(top)
    y_two = sol_two[...].astype(jnp.bfloat16)

    loads[1].wait()
    loads[2].wait()
    stacked_one = jnp.concatenate([y_two, jnp.zeros_like(y_two)], axis=0)
    by_core(lambda core: step_down(
        core, 0, 2, ROOT_SLABS, stacked_one, level_refs["one"], rhs_one, full_one, inv_one, sol_one
    ))
    y_one = sol_one[...].astype(jnp.bfloat16)

    loads[3].wait()
    stacked_root = jnp.concatenate([y_two, y_one], axis=0)
    by_core(lambda core: step_down(
        core, 1, 4, 0, stacked_root, level_refs["root"], rhs_root, full_root, inv_root, sol_root
    ))


def substitute(rhs_root, rhs_one, rhs_two, inv_root, inv_one, inv_two, placed):
    vmem = pl.BlockSpec(memory_space=pltpu.VMEM)
    hbm = pl.BlockSpec(memory_space=pl.ANY)
    bf16 = jnp.bfloat16

    def planes(*lead):
        return pltpu.VMEM((*lead, WIDTH, VECS), bf16)

    def level(nx):
        return [
            planes(nx * NY, NZ), planes(nx * NY, NZ), planes(nx * NY, NZ),
            planes(NY, NZ // 2), planes(NY, NZ // 2), planes(2, NY, NZ),
            planes(NY, NZ), planes(2, NZ // 2), planes(2, NZ),
            pltpu.VMEM((NZ, WIDTH, VECS), jnp.float32), planes(NZ - 1),
        ]

    sems = pltpu.SemaphoreType.DMA
    out = jax.ShapeDtypeStruct((WIDTH, VECS), jnp.float32)
    return pl.pallas_call(
        main_kernel,
        out_shape=(out, out, out),
        in_specs=[vmem] * 3 + [hbm] * 4,
        out_specs=(vmem,) * 3,
        scratch_shapes=[
            pltpu.VMEM(inv_root.shape, bf16),
            pltpu.VMEM(inv_one.shape, bf16),
            pltpu.VMEM(inv_two.shape, bf16),
            pltpu.VMEM(placed.shape, bf16),
            planes(NY, NZ, NC),
            planes(2 * NY, NZ, NC),
            planes(NX * NY, NZ, NC),
            *level(2),
            *level(4),
            sems((4,)),
            sems((2, 3, PARTS, NZ)),
            sems((2, 3, PARTS, 4)),
            sems((2, 3, PARTS, 4, 4)),
            sems((2, 3, PARTS, NX * NY)),
            sems((2, 2, PARTS, NZ)),
            sems((2, 2, PARTS, 4, 4)),
            sems((2, 2, PARTS, 4)),
            sems((2, 2, PARTS, NX * NY)),
        ],
        compiler_params=pltpu.CompilerParams(
            collective_id=0, has_side_effects=True, vmem_limit_bytes=60 * 2**20
        ),
    )(rhs_root, rhs_one, rhs_two, inv_root, inv_one, inv_two, placed)


def shards(
    rhs_root,
    rhs_one,
    rhs_two,
    inv_root,
    inv_one,
    inv_two,
    lower_one,
    lower_two,
    rows_one,
    rows_two,
    count_one,
    count_two,
):
    span = inv_root.shape[1] + inv_one.shape[1]
    placed = place(rows_two, rows_one, count_two, count_one, lower_two, lower_one, span)
    solved = substitute(rhs_root.T, rhs_one.T, rhs_two.T, inv_root, inv_one, inv_two, placed)
    return tuple(array.T for array in solved)


def solution(mesh):
    cut = P(None, ("leaf", "blk"))
    rows = P(("leaf", "blk"), None)
    return jax.shard_map(
        shards,
        mesh=mesh,
        in_specs=(cut, cut, cut, rows, rows, rows, rows, rows, P(), P(), P(), P()),
        out_specs=(cut, cut, cut),
        check_vma=False,
    )
```

time: 552 us -> 166 us (0.30)
  waiting for transfers between devices: 373 us -> 0 us
  Pallas kernels: 0 us -> 161 us
  other arithmetic: 106 us -> 0 us
  local copies, waits for them, and re-layouts: 25.5 us -> 4.12 us
  starting transfers between devices: 18 us -> 0 us
  matrix products: 14.1 us -> 0 us
  between operations: 14.4 us -> 0.65 us
    reduce_scatter x3 -> x0, waiting for transfers between devices: 184 us -> none  [solve_level(): lax.psum_scatter(local_sum, 'blk', scatter_dimension=1, tiled=True)]
    pallas_call x0 -> x2, Pallas kernels: none -> 161 us  [the longest x1 146 us: substitute(): pl.pallas_call(main_kernel, out_shape=(out, out, out), in_specs=[vmem] *...]
    all_gather x3 -> x0, waiting for transfers between devices: 132 us -> none  [solve_level(): lax.all_gather(part_sum.astype(jnp.bfloat16), 'blk', axis=1, tiled=True)]
    scatter-add x2 -> x0, other arithmetic: 96 us -> none  [the longest x1 49.6 us: shards(): jnp.zeros((vectors, width_root + width_one), jnp.float32).at[:, listed]]
    ppermute x9 -> x0, waiting for transfers between devices: 57.4 us -> none  [swapped(): lax.ppermute(array, axis, [(i, i ^ 1 << stride) for i in range(lax.axis_s...]
    ppermute x9 -> x0, starting transfers between devices: 17.5 us -> none  [swapped(): lax.ppermute(array, axis, [(i, i ^ 1 << stride) for i in range(lax.axis_s...]
    dot_general x5 -> x0, matrix products: 14.1 us -> none  [the longest x3 7.45 us: crossing(): lax.dot_general(rhs_full, inverse, (((1,), (1,)), ((), ())), preferred_el...]
    neg x2 -> x0, local copies, waits for them, and re-layouts: 11.1 us -> none  [the longest x1 5.57 us: shards(): root_pending = combined[:, :width_root].at[:, listed].add(-update_terms)]
  transfers between devices with their start and end apart: 15 -> 0, of which waited for: 15 -> 0; matrix products, arithmetic and copies ran while one was open for 2% -> 0% of each run, Pallas kernels for 0% -> 0%
where the time goes in v2:
time: 166 us
  Pallas kernels  161 us (97%)
  local copies, waits for them, and re-layouts  4.12 us (2%)
    pallas_call x1, Pallas kernels, substitute(): pl.pallas_call(main_kernel, out_shape=(out, out, out), in_specs=[vmem] *...  146 us
    pallas_call x1, Pallas kernels, place(): pl.pallas_call(place_kernel, out_shape=jax.ShapeDtypeStruct(result, jnp.b...  14.9 us
    unnamed x3, local copies, waits for them, and re-layouts  4.12 us

profile of v2, /device:TPU:1, one launch (start us, length us, event | category | flops | bytes accessed | tf_op | source)
XLA Modules:
  0.0 165.7 jit_solution(722054807365987266)
XLA Ops:
  0.6 14.9 %shard_map.139.placed_hbm = bf16[192,2,64,128]{3,2,1,0:T(8,128)(2,1)} custom-call(s32[4,8192]{1,0:T(4,128)} %rows_two_hbm.1, s32[2,8192]{1,0:T(2,128)} %rows_one_hbm.1, s32[4]{0:T(128)} %count_two.1, s32[2]{0:T(128)} %count_one.1, bf16[64,8192]{1,0:T(8,128)(2,1)} %lower_two_hbm.1, bf16[64,8192]{1,0:T(8,128)(2,1)} %lower_one_hbm.1), custom_call_target="tpu_custom_call" | custom-call | tf_op jit(solution)/shard_map/pallas_call | solution.py:94
  15.5 146.0 %shard_map.140 = (f32[64,128]{1,0:T(8,128)}, f32[64,128]{1,0:T(8,128)}, f32[64,128]{1,0:T(8,128)}) custom-call(f32[64,128]{1,0:T(8,128)} %bitcast.6, f32[64,128]{1,0:T(8,128)} %bitcast.7, f32[64,128]{1,0:T(8,128)} %bitcast.8, bf16[64,16384]{1,0:T(8,128)(2,1)} %inv_root_hbm.1, bf16[64,8192]{1,0:T(8,128)(2,1)} %inv_one_hbm.1, bf16[64,4096]{1,0:T(8,128)(2,1)} %inv_two_hbm.1, ...), custom_call_target="tpu_custom_call" | custom-call | tf_op jit(solution)/shard_map/pallas_call | solution.py:518
  161.6 1.4 copy.18
  162.9 1.4 copy.19
  164.3 1.4 copy.20

commit v3 on v0

v3 whole, which is shorter than its diff:
```python
import functools

import jax
import jax.numpy as jnp
from jax import lax
from jax.experimental import pallas as pl
from jax.experimental.pallas import tpu as pltpu
from jax.sharding import PartitionSpec as P

VECS = 128
WIDTH = 64
MESH = pl.DeviceIdType.MESH
NX, NY, NZ, NC = 4, 4, 8, 2
ROOT_SLABS = NX * NY


def main_kernel(
    rhs_root, rhs_one, rhs_two, inv_root_hbm, inv_one_hbm, inv_two_hbm,
    lower_two_hbm, lower_one_hbm, rows_two_hbm, rows_one_hbm, count_two, count_one,
    sol_root, sol_one, sol_two,
    inv_root, inv_one, inv_two, lower, rows_two, rows_one,
    found_two, found_one, index_two, index_one, source_two, source_one, placed_two, placed_one,
    full_two, full_one, full_root, solved, mine, theirs, both,
    *rest,
):
    level_refs = {"one": rest[:6], "root": rest[6:12]}
    local_sems, lower_sems, inv_sems, part_sems, z_sems, a_sems, b_sems, rz_sems, ra_sems, rb_sems = rest[12:]
    leaf = lax.axis_index("leaf")
    blk = lax.axis_index("blk")
    x, y = leaf // NY, leaf % NY
    z, c = blk // NC, blk % NC
    half, pair = x // 2, x % 2
    other = 1 - c
    length = lower_two_hbm.shape[1]

    def z_peer(at):
        return (leaf, at * NC + c)

    sibling = (leaf, z * NC + other)

    inverses = ((inv_two_hbm, inv_two), (inv_one_hbm, inv_one), (inv_root_hbm, inv_root))
    my_rows, their_rows = pl.ds(c * WIDTH, WIDTH), pl.ds(other * WIDTH, WIDTH)
    loads = [
        pltpu.make_async_copy(rows_two_hbm.at[pl.ds(x, 1)], rows_two, local_sems.at[0]),
        pltpu.make_async_copy(rows_one_hbm.at[pl.ds(half, 1)], rows_one, local_sems.at[1]),
        pltpu.make_async_copy(lower_two_hbm, lower.at[0, c], local_sems.at[2]),
        pltpu.make_async_copy(lower_one_hbm, lower.at[1, c], local_sems.at[3]),
        *[
            pltpu.make_async_copy(hbm, inverse.at[my_rows], local_sems.at[4 + level])
            for level, (hbm, inverse) in enumerate(inverses)
        ],
    ]
    for load in loads:
        load.start()

    barrier = pltpu.get_barrier_semaphore()
    greeted = [z_peer((z + o) % NZ) for o in range(1, NZ)]
    greeted += [(x * NY + (y + o) % NY, blk) for o in range(1, NY)]
    greeted += [((x + o) % NX * NY + y, blk) for o in range(1, NX)]
    greeted += [sibling]
    for device in greeted:
        pl.semaphore_signal(barrier, inc=1, device_id=device, device_id_type=MESH)

    def remote(source, target, sems, index, device):
        return pltpu.make_async_remote_copy(
            src_ref=source,
            dst_ref=target,
            send_sem=sems.at[(0, *index)],
            recv_sem=sems.at[(1, *index)],
            device_id=device,
            device_id_type=MESH,
        )

    def axes_of(core, nx):
        mine_x = {1: 0, 2: pair, 4: x}[nx]

        def x_peer(o):
            to = half * 2 + (pair + o) % 2 if nx == 2 else (x + o) % NX
            return (to * NY + y, blk)

        def y_peer(o):
            return (x * NY + (y + o) % NY, blk)

        along_x, along_y = (nx, x_peer), (NY, y_peer)
        first, second = (along_y, along_x) if core == 0 else (along_x, along_y)

        def slab(oa, ob):
            ox, oy = (ob, oa) if core == 0 else (oa, ob)
            return (mine_x + ox) % nx * NY + (y + oy) % NY

        return first, second, slab

    def by_core(body):
        for core in range(NC):
            pl.when(c == core)(functools.partial(body, core))

    lists = (
        (rows_two, count_two, x, found_two, index_two, source_two, placed_two),
        (rows_one, count_one, half, found_one, index_one, source_one, placed_one),
    )

    def index_copy(which):
        return pltpu.make_async_copy(lists[which][3], lists[which][4], local_sems.at[7 + which])

    def invert(which):
        rows, counts, at, found, _, _, placed = lists[which]
        blocks, step = placed.shape[0], 1024
        count = counts[at]

        def body(i, total):
            row = rows[:, pl.ds(pl.multiple_of(i * step, step), step)]
            entry = lax.broadcasted_iota(jnp.int32, (1, step), 1) + i * step + 1
            block = jnp.where(entry <= count, row // 128, -1)
            within = row % 128 - c * WIDTH
            here = lax.broadcasted_iota(jnp.int32, (blocks, step), 0) == block
            mine = lax.broadcasted_iota(jnp.int32, (WIDTH, step), 0) == within
            upper = jnp.where(mine, (entry // 128).astype(jnp.float32), 0.0)
            lower_part = jnp.where(mine, (entry % 128).astype(jnp.float32), 0.0)
            digits = jnp.concatenate([upper, lower_part], axis=0).astype(jnp.bfloat16)
            return total + lax.dot_general(
                jnp.where(here, 1.0, 0.0).astype(jnp.bfloat16), digits, (((1,), (1,)), ((), ())),
                preferred_element_type=jnp.float32,
            )

        total = lax.fori_loop(0, length // step, body, jnp.zeros((blocks, 2 * WIDTH), jnp.float32))
        entry = (total[:, :WIDTH] * 128.0 + total[:, WIDTH:]).astype(jnp.int32)
        found[...] = jnp.clip(jnp.where(entry > 0, entry - 1, length), 0, length)
        index_copy(which).start()

    def lower_copy(which):
        hbm = (lower_two_hbm, lower_one_hbm)[which]
        return remote(hbm, lower.at[which, c], lower_sems, (which,), sibling)

    def lower_arrival(which):
        return remote(lower.at[which, other], lower.at[which, other], lower_sems, (which,), sibling)

    def inverse_copy(level):
        hbm, inverse = inverses[level]
        return remote(hbm, inverse.at[my_rows], inv_sems, (level,), sibling)

    def inverse_here(level):
        inverse = inverses[level][1]
        loads[4 + level].wait()
        remote(inverse.at[their_rows], inverse.at[their_rows], inv_sems, (level,), sibling).wait_recv()

    def turn(which):
        source, step = lists[which][5], 512
        loads[2 + which].wait()
        lower_arrival(which).wait_recv()

        def body(i, carry):
            cols = pl.ds(pl.multiple_of(i * step, step), step)
            both = jnp.concatenate([lower[which, 0, :, cols], lower[which, 1, :, cols]], axis=0)
            source[cols, :] = both.astype(jnp.float32).T
            return carry

        lax.fori_loop(0, length // step, body, 0)
        source[length:, :] = jnp.zeros((source.shape[0] - length, 2 * WIDTH), jnp.float32)

    def fetch(which, start, stop):
        _, _, _, _, index, source, placed = lists[which]

        def body(block, carry):
            picked = [source[pl.ds(index[block, k], 1), :] for k in range(WIDTH)]
            placed[block] = jnp.concatenate(picked, axis=0).astype(jnp.bfloat16)
            return carry

        lax.fori_loop(start, stop, body, 0)

    def fetches(which, start, stop, step):
        return [functools.partial(fetch, which, at, at + step) for at in range(start, stop, step)]

    def run(queue, count):
        for _ in range(min(count, len(queue))):
            queue.pop(0)()

    def gather(core, level, nx, full, out, sent, queue, beside):
        (na, a_peer), (nb, b_peer), slab_at = axes_of(core, nx)
        inverse = inverses[level][1]
        wide = NZ * NC * WIDTH
        ring = na == nb == 4
        low, high, whole = slice(0, NZ // 2), slice(NZ // 2, NZ), slice(0, NZ)

        def start(make):
            make().start()
            sent.append(make)

        def flush():
            while sent:
                sent.pop(0)().wait_send()

        def z_copy(o, arrival=False):
            at = (z + NZ - o) % NZ if arrival else z
            block = full.at[slab_at(0, 0), at, c]
            return remote(block, block, z_sems, (level, o), z_peer((z + o) % NZ))

        def plane(oa, ob, zs=whole):
            return full.at[slab_at(oa, ob), zs, c]

        def a_copy(oa, arrival=False):
            block = plane(na - oa if arrival else 0, 0)
            return remote(block, block, a_sems, (level, oa), a_peer(oa))

        def b_copy(oa, ob, arrival=False):
            block = plane(oa, nb - ob if arrival else 0)
            return remote(block, block, b_sems, (level, oa, ob), b_peer(ob))

        def b_half(oa, kind, arrival=False):
            block = plane(oa, 2 if arrival else (3, 0, 1)[kind], (low, None, high)[kind])
            return remote(block, block, b_sems, (level, oa, kind), b_peer((1, None, 3)[kind]))

        def b_send(oa):
            for ob in (1, 3) if ring else range(1, nb):
                start(functools.partial(b_copy, oa, ob))

        def dot(oa, ob):
            slab = slab_at(oa, ob)
            return jnp.dot(
                inverse[:, pl.ds(pl.multiple_of(slab * wide, wide), wide)],
                full[slab].reshape(wide, VECS),
                preferred_element_type=jnp.float32,
            )

        for o in range(1, NZ):
            start(functools.partial(z_copy, o))
        run(queue, beside[0])
        for o in range(1, NZ):
            z_copy(o, True).wait_recv()
        earlier = len(sent)
        for oa in range(1, na):
            start(functools.partial(a_copy, oa))
        b_send(0)
        for make in [sent.pop(0) for _ in range(earlier)]:
            make().wait_send()
        run(queue, beside[1])
        inverse_here(level)
        total = dot(0, 0)
        for oa in range(1, na):
            a_copy(oa, True).wait_recv()
            b_send(na - oa)
        run(queue, beside[2])
        for oa in range(1, na):
            total += dot(oa, 0)
        for oa in [0, *range(na - 1, 0, -1)]:
            if ring:
                for ob, kind in ((1, 0), (3, 2)):
                    b_copy(oa, ob, True).wait_recv()
                    start(functools.partial(b_half, oa, kind))
            else:
                for ob in range(1, nb):
                    b_copy(oa, ob, True).wait_recv()
            run(queue, beside[3])
            for ob in (1, 3) if ring else range(1, nb):
                total += dot(oa, ob)
        if ring:
            for oa in [0, *range(na - 1, 0, -1)]:
                b_half(oa, 0, True).wait_recv()
                b_half(oa, 2, True).wait_recv()
                total += dot(oa, 2)
        mine[level] = total
        partial = remote(mine.at[level], theirs.at[level], part_sems, (level,), sibling)
        partial.start()
        flush()
        partial.wait()
        total = mine[level] + theirs[level]
        both[...] = total
        out[...] = both[my_rows]
        if level < 2:
            solved[level] = total.astype(jnp.bfloat16)

    def reduce(core, level, nx, terms, refs, sent, queue, beside):
        sums, ra, totals, rb, whole, landed = refs
        (na, a_peer), (nb, b_peer), slab_at = axes_of(core, nx)

        def start(make):
            make().start()
            sent.append(make)

        def a_copy(oa, ob):
            return remote(sums.at[slab_at(oa, ob)], ra.at[oa - 1, ob], ra_sems, (level, oa, ob), a_peer(oa))

        def b_copy(ob):
            return remote(totals.at[ob], rb.at[ob - 1], rb_sems, (level, ob), b_peer(ob))

        def z_copy(o):
            return remote(totals.at[0, (z + o) % NZ], landed.at[o - 1], rz_sems, (level, o), z_peer((z + o) % NZ))

        ring = na == nb == 4
        low, high = slice(0, NZ // 2), slice(NZ // 2, NZ)

        def a_half(kind, ob):
            zs = (low, high)[kind]
            target = ra.at[1, ob, zs]
            return remote(sums.at[slab_at(2, ob), zs], target, ra_sems, (level, 2 * kind, ob), a_peer((1, 3)[kind]))

        order = [*range(1, nb), 0]
        if ring:
            for ob in order:
                slab = slab_at(2, ob)
                sums[slab] = terms(slab).astype(jnp.bfloat16)
                start(functools.partial(a_half, 0, ob))
                start(functools.partial(a_half, 1, ob))
            for ob in order:
                for kind, oa in ((0, 1), (1, 3)):
                    slab = slab_at(oa, ob)
                    value = terms(slab)
                    a_half(kind, ob).wait_recv()
                    zs = (low, high)[kind]
                    extra = ra[1, ob, zs].astype(jnp.float32)
                    halves = [value[: NZ // 2], value[NZ // 2 :]]
                    halves[kind] = halves[kind] + extra
                    sums[slab] = jnp.concatenate(halves, axis=0).astype(jnp.bfloat16)
                    start(functools.partial(a_copy, oa, ob))
        else:
            for ob in order:
                for oa in range(1, na):
                    slab = slab_at(oa, ob)
                    sums[slab] = terms(slab).astype(jnp.bfloat16)
                    start(functools.partial(a_copy, oa, ob))
        run(queue, beside[0])
        for ob in order:
            value = terms(slab_at(0, ob))
            for oa in (1, 3) if ring else range(1, na):
                a_copy(oa, ob).wait_recv()
                value += ra[oa - 1, ob].astype(jnp.float32)
            if ob:
                totals[ob] = value.astype(jnp.bfloat16)
                start(functools.partial(b_copy, ob))
            else:
                whole[...] = value
        run(queue, beside[1])
        value = whole[...]
        for ob in range(1, nb):
            b_copy(ob).wait_recv()
            value += rb[ob - 1].astype(jnp.float32)
        whole[...] = value
        totals[0] = value.astype(jnp.bfloat16)
        for o in range(1, NZ):
            start(functools.partial(z_copy, o))
        run(queue, beside[2])
        value = whole[z]
        for o in range(1, NZ):
            z_copy(o).wait_recv()
            value += landed[o - 1].astype(jnp.float32)
        return value

    def of_two(slab, first):
        blocks = placed_two[pl.ds((first + slab) * NZ, NZ)].reshape(NZ * WIDTH, 2 * WIDTH)
        return jnp.dot(blocks, solved[0], preferred_element_type=jnp.float32)

    def of_one(slab):
        blocks = placed_one[pl.ds(slab * NZ, NZ)].reshape(NZ * WIDTH, 2 * WIDTH)
        return jnp.dot(blocks, solved[1], preferred_element_type=jnp.float32)

    full_two[y, z, c] = rhs_two[...].astype(jnp.bfloat16)
    for full in (full_two, full_one, full_root):
        def blank(slab, carry, full=full):
            full[slab, :, other] = jnp.zeros((NZ, WIDTH, VECS), jnp.bfloat16)
            return carry

        lax.fori_loop(0, full.shape[0], blank, 0)
    pl.semaphore_wait(barrier, len(greeted))
    root_blocks = placed_one.shape[0]

    def start_two():
        lower_copy(0).start()
        inverse_copy(0).start()
        loads[0].wait()
        invert(0)

    def start_one():
        lower_copy(1).start()
        inverse_copy(1).start()
        inverse_copy(2).start()
        loads[1].wait()
        invert(1)

    def wait_index(which):
        index_copy(which).wait()

    def top(core):
        sent = []
        queue = [
            start_two, lambda: turn(0), lambda: wait_index(0),
            *fetches(0, root_blocks, placed_two.shape[0], 16),
        ]
        gather(core, 0, 1, full_two, sol_two, sent, queue, (1, 4, 2, 1))
        run(queue, len(queue))

    by_core(top)

    def middle(core):
        sent = []
        queue = [
            start_one, lambda: turn(1), lambda: wait_index(1),
            *fetches(0, 0, root_blocks, 16), *fetches(1, 0, root_blocks, 16),
        ]
        moved = reduce(
            core, 0, 2, lambda slab: of_two(slab, ROOT_SLABS).reshape(NZ, WIDTH, VECS), level_refs["one"], sent, queue,
            (4, 1, 3),
        )
        full_one[pair * NY + y, z, c] = (rhs_one[...] - moved).astype(jnp.bfloat16)
        gather(core, 1, 2, full_one, sol_one, sent, queue, (3, 2, 1, 1))
        run(queue, len(queue))

    by_core(middle)

    def bottom(core):
        sent = []
        moved = reduce(
            core, 1, 4, lambda slab: (of_two(slab, 0) + of_one(slab)).reshape(NZ, WIDTH, VECS), level_refs["root"],
            sent, [], (0, 0, 0),
        )
        full_root[x * NY + y, z, c] = (rhs_root[...] - moved).astype(jnp.bfloat16)
        gather(core, 2, 4, full_root, sol_root, sent, [], (0, 0, 0, 0))

    by_core(bottom)
    for which in range(2):
        lower_copy(which).wait_send()
    for level in range(3):
        inverse_copy(level).wait_send()


def substitute(rhs_root, rhs_one, rhs_two, inv_root, inv_one, inv_two, lower_two, lower_one, rows_two, rows_one, count_two, count_one):
    vmem = pl.BlockSpec(memory_space=pltpu.VMEM)
    smem = pl.BlockSpec(memory_space=pltpu.SMEM)
    hbm = pl.BlockSpec(memory_space=pl.ANY)
    bf16 = jnp.bfloat16
    length = lower_two.shape[1]
    blocks_one = inv_root.shape[1] // (NC * WIDTH)
    blocks_two = blocks_one + inv_one.shape[1] // (NC * WIDTH)

    def planes(*lead):
        return pltpu.VMEM((*lead, WIDTH, VECS), bf16)

    def level(nx):
        return [
            planes(nx * NY, NZ), planes(3, NY, NZ), planes(NY, NZ), planes(3, NZ),
            pltpu.VMEM((NZ, WIDTH, VECS), jnp.float32), planes(NZ - 1),
        ]

    sems = pltpu.SemaphoreType.DMA
    out = jax.ShapeDtypeStruct((WIDTH, VECS), jnp.float32)
    return pl.pallas_call(
        main_kernel,
        out_shape=(out, out, out),
        in_specs=[vmem] * 3 + [hbm] * 7 + [smem] * 2,
        out_specs=(vmem,) * 3,
        scratch_shapes=[
            *[pltpu.VMEM((2 * WIDTH, inverse.shape[1]), bf16) for inverse in (inv_root, inv_one, inv_two)],
            pltpu.VMEM((2, NC, WIDTH, length), bf16),
            pltpu.VMEM((1, length), jnp.int32),
            pltpu.VMEM((1, length), jnp.int32),
            pltpu.VMEM((blocks_two, WIDTH), jnp.int32),
            pltpu.VMEM((blocks_one, WIDTH), jnp.int32),
            pltpu.SMEM((blocks_two, WIDTH), jnp.int32),
            pltpu.SMEM((blocks_one, WIDTH), jnp.int32),
            pltpu.VMEM((length + 8, 2 * WIDTH), jnp.float32),
            pltpu.VMEM((length + 8, 2 * WIDTH), jnp.float32),
            pltpu.VMEM((blocks_two, WIDTH, 2 * WIDTH), bf16),
            pltpu.VMEM((blocks_one, WIDTH, 2 * WIDTH), bf16),
            planes(NY, NZ, NC),
            planes(2 * NY, NZ, NC),
            planes(NX * NY, NZ, NC),
            pltpu.VMEM((2, 2 * WIDTH, VECS), bf16),
            pltpu.VMEM((3, 2 * WIDTH, VECS), jnp.float32),
            pltpu.VMEM((3, 2 * WIDTH, VECS), jnp.float32),
            pltpu.VMEM((2 * WIDTH, VECS), jnp.float32),
            *level(2),
            *level(4),
            sems((9,)),
            sems((2, 2)),
            sems((2, 3)),
            sems((2, 3)),
            sems((2, 3, NZ)),
            sems((2, 3, 4)),
            sems((2, 3, 4, 4)),
            sems((2, 2, NZ)),
            sems((2, 2, 4, 4)),
            sems((2, 2, 4)),
        ],
        compiler_params=pltpu.CompilerParams(
            collective_id=0, has_side_effects=True, vmem_limit_bytes=60 * 2**20
        ),
    )(rhs_root, rhs_one, rhs_two, inv_root, inv_one, inv_two, lower_two, lower_one, rows_two, rows_one, count_two, count_one)


def hand_over_kernel(*refs):
    for given, out in zip(refs[:3], refs[3:]):
        out[...] = given[...]


def hand_over(arrays):
    vmem = pl.BlockSpec(memory_space=pltpu.VMEM)
    return pl.pallas_call(
        hand_over_kernel,
        out_shape=tuple(jax.ShapeDtypeStruct(array.shape, array.dtype) for array in arrays),
        in_specs=[vmem] * 3,
        out_specs=(vmem,) * 3,
    )(*arrays)


def shards(
    rhs_root,
    rhs_one,
    rhs_two,
    inv_root,
    inv_one,
    inv_two,
    lower_one,
    lower_two,
    rows_one,
    rows_two,
    count_one,
    count_two,
):
    solved = substitute(
        rhs_root.T, rhs_one.T, rhs_two.T, inv_root, inv_one, inv_two,
        lower_two, lower_one, rows_two, rows_one, count_two, count_one,
    )
    return tuple(array.T for array in hand_over(solved))


def solution(mesh):
    cut = P(None, ("leaf", "blk"))
    rows = P(("leaf", "blk"), None)
    return jax.shard_map(
        shards,
        mesh=mesh,
        in_specs=(cut, cut, cut, rows, rows, rows, rows, rows, P(), P(), P(), P()),
        out_specs=(cut, cut, cut),
        check_vma=False,
    )
```

time: 552 us -> 122 us (0.22)
  waiting for transfers between devices: 373 us -> 0 us
  Pallas kernels: 0 us -> 121 us
  other arithmetic: 106 us -> 0 us
  local copies, waits for them, and re-layouts: 25.5 us -> 0 us
  starting transfers between devices: 18 us -> 0 us
  matrix products: 14.1 us -> 0 us
  between operations: 14.4 us -> 0.64 us
    reduce_scatter x3 -> x0, waiting for transfers between devices: 184 us -> none  [solve_level(): lax.psum_scatter(local_sum, 'blk', scatter_dimension=1, tiled=True)]
    all_gather x3 -> x0, waiting for transfers between devices: 132 us -> none  [solve_level(): lax.all_gather(part_sum.astype(jnp.bfloat16), 'blk', axis=1, tiled=True)]
    pallas_call x0 -> x2, Pallas kernels: none -> 121 us  [the longest x1 119 us: substitute(): pl.pallas_call(main_kernel, out_shape=(out, out, out), in_specs=[vmem] *...]
    scatter-add x2 -> x0, other arithmetic: 96 us -> none  [the longest x1 49.6 us: shards(): jnp.zeros((vectors, width_root + width_one), jnp.float32).at[:, listed]]
    ppermute x9 -> x0, waiting for transfers between devices: 57.4 us -> none  [swapped(): lax.ppermute(array, axis, [(i, i ^ 1 << stride) for i in range(lax.axis_s...]
    ppermute x9 -> x0, starting transfers between devices: 17.5 us -> none  [swapped(): lax.ppermute(array, axis, [(i, i ^ 1 << stride) for i in range(lax.axis_s...]
    dot_general x5 -> x0, matrix products: 14.1 us -> none  [the longest x3 7.45 us: crossing(): lax.dot_general(rhs_full, inverse, (((1,), (1,)), ((), ())), preferred_el...]
    neg x2 -> x0, local copies, waits for them, and re-layouts: 11.1 us -> none  [the longest x1 5.57 us: shards(): root_pending = combined[:, :width_root].at[:, listed].add(-update_terms)]
  transfers between devices with their start and end apart: 15 -> 0, of which waited for: 15 -> 0; matrix products, arithmetic and copies ran while one was open for 2% -> 0% of each run, Pallas kernels for 0% -> 0%
where the time goes in v3:
time: 122 us; the launch traced here: 121 us
  Pallas kernels  121 us (99%)
    pallas_call x1, Pallas kernels, substitute(): pl.pallas_call(main_kernel, out_shape=(out, out, out), in_specs=[vmem] *...  119 us

profile of v3, /device:TPU:1, one launch (start us, length us, event | category | flops | bytes accessed | tf_op | source)
XLA Modules:
  0.0 121.4 jit_solution(4375020649979570699)
XLA Ops:
  0.6 119.3 %shard_map.139 = (f32[64,128]{1,0:T(8,128)}, f32[64,128]{1,0:T(8,128)}, f32[64,128]{1,0:T(8,128)}) custom-call(f32[64,128]{1,0:T(8,128)} %bitcast.6, f32[64,128]{1,0:T(8,128)} %bitcast.7, f32[64,128]{1,0:T(8,128)} %bitcast.8, bf16[64,16384]{1,0:T(8,128)(2,1)} %inv_root_hbm.1, bf16[64,8192]{1,0:T(8,128)(2,1)} %inv_one_hbm.1, bf16[64,4096]{1,0:T(8,128)(2,1)} %inv_two_hbm.1, ...), custom_call_target="tpu_custom_call" | custom-call | tf_op jit(solution)/shard_map/pallas_call | solution.py:444
  119.9 1.4 %shard_map.140 = (f32[64,128]{1,0:T(8,128)}, f32[64,128]{1,0:T(8,128)}, f32[64,128]{1,0:T(8,128)}) custom-call(f32[64,128]{1,0:T(8,128)} %get-tuple-element.9.refs_0_, f32[64,128]{1,0:T(8,128)} %get-tuple-element.10.refs_1_, f32[64,128]{1,0:T(8,128)} %get-tuple-element.11.refs_2_), custom_call_target="tpu_custom_call" | custom-call | tf_op jit(solution)/shard_map/pallas_call | solution.py:495

commit v4 on v3

--- a/solution.py
+++ b/solution.py
@@ -12,6 +12,7 @@
 MESH = pl.DeviceIdType.MESH
 NX, NY, NZ, NC = 4, 4, 8, 2
 ROOT_SLABS = NX * NY
+PARTS = 2
 
 
 def main_kernel(
@@ -84,11 +85,11 @@
         along_x, along_y = (nx, x_peer), (NY, y_peer)
         first, second = (along_y, along_x) if core == 0 else (along_x, along_y)
 
-        def slab(oa, ob):
+        def offsets(oa, ob):
             ox, oy = (ob, oa) if core == 0 else (oa, ob)
-            return (mine_x + ox) % nx * NY + (y + oy) % NY
-
-        return first, second, slab
+            return (mine_x + ox) % nx, (y + oy) % NY
+
+        return first, second, offsets
 
     def by_core(body):
         for core in range(NC):
@@ -174,93 +175,31 @@
         for _ in range(min(count, len(queue))):
             queue.pop(0)()
 
-    def gather(core, level, nx, full, out, sent, queue, beside):
-        (na, a_peer), (nb, b_peer), slab_at = axes_of(core, nx)
-        inverse = inverses[level][1]
+    def part_of(h):
+        return slice(h * WIDTH // PARTS, (h + 1) * WIDTH // PARTS)
+
+    def started(sent, make):
+        make().start()
+        sent.append(make)
+
+    def flush(sent):
+        while sent:
+            sent.pop(0)().wait_send()
+
+    def product(level, full, at_x, at_y):
         wide = NZ * NC * WIDTH
-        ring = na == nb == 4
-        low, high, whole = slice(0, NZ // 2), slice(NZ // 2, NZ), slice(0, NZ)
-
-        def start(make):
-            make().start()
-            sent.append(make)
-
-        def flush():
-            while sent:
-                sent.pop(0)().wait_send()
-
-        def z_copy(o, arrival=False):
-            at = (z + NZ - o) % NZ if arrival else z
-            block = full.at[slab_at(0, 0), at, c]
-            return remote(block, block, z_sems, (level, o), z_peer((z + o) % NZ))
-
-        def plane(oa, ob, zs=whole):
-            return full.at[slab_at(oa, ob), zs, c]
-
-        def a_copy(oa, arrival=False):
-            block = plane(na - oa if arrival else 0, 0)
-            return remote(block, block, a_sems, (level, oa), a_peer(oa))
-
-        def b_copy(oa, ob, arrival=False):
-            block = plane(oa, nb - ob if arrival else 0)
-            return remote(block, block, b_sems, (level, oa, ob), b_peer(ob))
-
-        def b_half(oa, kind, arrival=False):
-            block = plane(oa, 2 if arrival else (3, 0, 1)[kind], (low, None, high)[kind])
-            return remote(block, block, b_sems, (level, oa, kind), b_peer((1, None, 3)[kind]))
-
-        def b_send(oa):
-            for ob in (1, 3) if ring else range(1, nb):
-                start(functools.partial(b_copy, oa, ob))
-
-        def dot(oa, ob):
-            slab = slab_at(oa, ob)
-            return jnp.dot(
-                inverse[:, pl.ds(pl.multiple_of(slab * wide, wide), wide)],
-                full[slab].reshape(wide, VECS),
-                preferred_element_type=jnp.float32,
-            )
-
-        for o in range(1, NZ):
-            start(functools.partial(z_copy, o))
-        run(queue, beside[0])
-        for o in range(1, NZ):
-            z_copy(o, True).wait_recv()
-        earlier = len(sent)
-        for oa in range(1, na):
-            start(functools.partial(a_copy, oa))
-        b_send(0)
-        for make in [sent.pop(0) for _ in range(earlier)]:
-            make().wait_send()
-        run(queue, beside[1])
-        inverse_here(level)
-        total = dot(0, 0)
-        for oa in range(1, na):
-            a_copy(oa, True).wait_recv()
-            b_send(na - oa)
-        run(queue, beside[2])
-        for oa in range(1, na):
-            total += dot(oa, 0)
-        for oa in [0, *range(na - 1, 0, -1)]:
-            if ring:
-                for ob, kind in ((1, 0), (3, 2)):
-                    b_copy(oa, ob, True).wait_recv()
-                    start(functools.partial(b_half, oa, kind))
-            else:
-                for ob in range(1, nb):
-                    b_copy(oa, ob, True).wait_recv()
-            run(queue, beside[3])
-            for ob in (1, 3) if ring else range(1, nb):
-                total += dot(oa, ob)
-        if ring:
-            for oa in [0, *range(na - 1, 0, -1)]:
-                b_half(oa, 0, True).wait_recv()
-                b_half(oa, 2, True).wait_recv()
-                total += dot(oa, 2)
+        slab = at_x * NY + at_y
+        return jnp.dot(
+            inverses[level][1][:, pl.ds(pl.multiple_of(slab * wide, wide), wide)],
+            full[at_x, at_y].reshape(wide, VECS),
+            preferred_element_type=jnp.float32,
+        )
+
+    def conclude(level, total, out, sent):
         mine[level] = total
         partial = remote(mine.at[level], theirs.at[level], part_sems, (level,), sibling)
         partial.start()
-        flush()
+        flush(sent)
         partial.wait()
         total = mine[level] + theirs[level]
         both[...] = total
@@ -268,97 +207,243 @@
         if level < 2:
             solved[level] = total.astype(jnp.bfloat16)
 
-    def reduce(core, level, nx, terms, refs, sent, queue, beside):
+    def top(core):
+        sent = []
+
+        def z_copy(o, arrival=False):
+            at = (z + NZ - o) % NZ if arrival else z
+            block = full_two.at[0, y, at, c] if core == 0 else full_two.at[0, :, at, c]
+            return remote(block, block, z_sems, (0, 0, o), z_peer((z + o) % NZ))
+
+        def y_copy(o, arrival=False):
+            at = (y + NY - o) % NY if arrival else y
+            block = full_two.at[0, at, :, c] if core == 0 else full_two.at[0, at, z, c]
+            return remote(block, block, a_sems, (0, 0, o), (x * NY + (y + o) % NY, blk))
+
+        near, far = ((z_copy, NZ), (y_copy, NY))[:: 1 if core == 0 else -1]
+        for o in range(1, near[1]):
+            started(sent, functools.partial(near[0], o))
+        start_two()
+        for o in range(1, near[1]):
+            near[0](o, True).wait_recv()
+        for o in range(1, far[1]):
+            started(sent, functools.partial(far[0], o))
+        turn(0)
+        wait_index(0)
+        fetch(0, root_blocks, placed_two.shape[0])
+        inverse_here(0)
+        for o in range(1, far[1]):
+            far[0](o, True).wait_recv()
+        total = jnp.zeros((2 * WIDTH, VECS), jnp.float32)
+        for at_y in range(NY):
+            total += product(0, full_two, 0, at_y)
+        conclude(0, total, sol_two, sent)
+
+    def level_down(level, nx, terms, refs, rhs, full, out, queue, beside):
         sums, ra, totals, rb, whole, landed = refs
-        (na, a_peer), (nb, b_peer), slab_at = axes_of(core, nx)
-
-        def start(make):
-            make().start()
-            sent.append(make)
-
-        def a_copy(oa, ob):
-            return remote(sums.at[slab_at(oa, ob)], ra.at[oa - 1, ob], ra_sems, (level, oa, ob), a_peer(oa))
-
-        def b_copy(ob):
-            return remote(totals.at[ob], rb.at[ob - 1], rb_sems, (level, ob), b_peer(ob))
-
-        def z_copy(o):
-            return remote(totals.at[0, (z + o) % NZ], landed.at[o - 1], rz_sems, (level, o), z_peer((z + o) % NZ))
-
-        ring = na == nb == 4
-        low, high = slice(0, NZ // 2), slice(NZ // 2, NZ)
-
-        def a_half(kind, ob):
-            zs = (low, high)[kind]
-            target = ra.at[1, ob, zs]
-            return remote(sums.at[slab_at(2, ob), zs], target, ra_sems, (level, 2 * kind, ob), a_peer((1, 3)[kind]))
-
-        order = [*range(1, nb), 0]
+        sent, last = [], []
+        plan = [axes_of(h, nx) for h in range(PARTS)]
+        ring = nx == 4
+        low, high, every = slice(0, NZ // 2), slice(NZ // 2, NZ), slice(None)
+
+        def a_copy(h, oa, zs, target, to):
+            (_, a_peer), (nb, _), _ = plan[h]
+            at = (slice(0, nb), zs, part_of(h))
+            return remote(
+                sums.at[(oa - 1, *at)], ra.at[(target - 1, *at)], ra_sems,
+                (level, h, oa, {low: 0, high: 1, every: 0}[zs]), a_peer(to),
+            )
+
+        def b_copy(ob, h):
+            return remote(
+                totals.at[ob, :, part_of(h)], rb.at[ob - 1, :, part_of(h)], rb_sems, (level, h, ob), plan[h][1][1](ob)
+            )
+
+        def z_copy(o, h):
+            return remote(
+                totals.at[0, (z + o) % NZ, part_of(h)], landed.at[o - 1, part_of(h)], rz_sems, (level, h, o),
+                z_peer((z + o) % NZ),
+            )
+
+        def make(h, oa):
+            for ob in range(plan[h][1][0]):
+                sums[oa - 1, ob, :, part_of(h)] = terms(plan[h][2](oa, ob), part_of(h)).astype(jnp.bfloat16)
+
+        def a_start():
+            if not ring:
+                for h in range(PARTS):
+                    for oa in range(1, plan[h][0][0]):
+                        make(h, oa)
+                        started(sent, functools.partial(a_copy, h, oa, every, oa, oa))
+                return
+            for h in range(PARTS):
+                make(h, 2)
+                started(sent, functools.partial(a_copy, h, 2, low, 2, 1))
+                started(sent, functools.partial(a_copy, h, 2, high, 2, 3))
+            for h in range(PARTS):
+                for oa, zs in ((1, high), (3, low)):
+                    make(h, oa)
+                    started(sent, functools.partial(a_copy, h, oa, zs, oa, oa))
+
+        def a_middle(h):
+            if ring:
+                for oa, zs, to in ((1, low, 1), (3, high, 3)):
+                    a_copy(h, 2, zs, 2, to).wait_recv()
+                    at = (slice(0, NY), zs, part_of(h))
+                    joined = sums[(oa - 1, *at)].astype(jnp.float32) + ra[(1, *at)].astype(jnp.float32)
+                    sums[(oa - 1, *at)] = joined.astype(jnp.bfloat16)
+                    started(sent, functools.partial(a_copy, h, oa, zs, oa, oa))
+
+        def a_close(h):
+            (na, _), (nb, _), offsets = plan[h]
+            rows = part_of(h)
+            for oa in (1, 3) if ring else range(1, na):
+                for zs in (low, high) if ring else (every,):
+                    a_copy(h, oa, zs, oa, oa).wait_recv()
+            for ob in [*range(1, nb), 0]:
+                value = terms(offsets(0, ob), rows)
+                for oa in (1, 3) if ring else range(1, na):
+                    value += ra[oa - 1, ob, :, rows].astype(jnp.float32)
+                if ob:
+                    totals[ob, :, rows] = value.astype(jnp.bfloat16)
+                    started(sent, functools.partial(b_copy, ob, h))
+                else:
+                    whole[:, rows] = value
+
+        def b_close(h):
+            rows = part_of(h)
+            value = whole[:, rows]
+            for ob in range(1, plan[h][1][0]):
+                b_copy(ob, h).wait_recv()
+                value += rb[ob - 1, :, rows].astype(jnp.float32)
+            whole[:, rows] = value
+            totals[0, :, rows] = value.astype(jnp.bfloat16)
+            for o in range(1, NZ):
+                started(sent, functools.partial(z_copy, o, h))
+
+        def z_close(h):
+            rows = part_of(h)
+            value = whole[z, rows]
+            for o in range(1, NZ):
+                z_copy(o, h).wait_recv()
+                value += landed[o - 1, rows].astype(jnp.float32)
+            at_x, at_y = plan[h][2](0, 0)
+            full[at_x, at_y, z, c, rows] = (rhs[rows] - value).astype(jnp.bfloat16)
+            for o in range(1, NZ):
+                started(sent, functools.partial(own_copy, o, h))
+
+        def own_copy(o, h, arrival=False):
+            at = (z + NZ - o) % NZ if arrival else z
+            block = full.at[(*plan[h][2](0, 0), at, c, part_of(h))]
+            return remote(block, block, z_sems, (level + 1, h, o), z_peer((z + o) % NZ))
+
+        def near_copy(oa, h, arrival=False):
+            (na, a_peer), _, offsets = plan[h]
+            block = full.at[(*offsets(na - oa if arrival else 0, 0), every, c, part_of(h))]
+            return remote(block, block, a_sems, (level + 1, h, oa), a_peer(oa))
+
+        def far_copy(h, origin, zs, to):
+            (_, b_peer), offsets = plan[h][1:]
+            at_x, at_y = offsets(0, origin)
+            line = (at_x, every) if h == 0 else (every, at_y)
+            block = full.at[(*line, zs, c, part_of(h))]
+            kind = to if origin == 0 else 2
+            return remote(
+                block, block, b_sems, (level + 1, h, kind, {low: 0, high: 1, every: 0}[zs]), b_peer(to)
+            )
+
+        def far_arrival(h, ob, zs, by):
+            (nb, b_peer), offsets = plan[h][1:]
+            at_x, at_y = offsets(0, ob)
+            line = (at_x, every) if h == 0 else (every, at_y)
+            block = full.at[(*line, zs, c, part_of(h))]
+            return remote(block, block, b_sems, (level + 1, h, by, {low: 0, high: 1, every: 0}[zs]), b_peer(0 if nb < 2 else 1))
+
+        def near_start(h):
+            for o in range(1, NZ):
+                own_copy(o, h, True).wait_recv()
+            for oa in range(1, plan[h][0][0]):
+                started(sent, functools.partial(near_copy, oa, h))
+
+        def far_start(h):
+            for oa in range(1, plan[h][0][0]):
+                near_copy(oa, h, True).wait_recv()
+            if ring:
+                for to, zs in ((1, low), (3, high), (1, high), (3, low)):
+                    started(last, functools.partial(far_copy, h, 0, zs, to))
+            else:
+                for ob in range(1, plan[h][1][0]):
+                    started(last, functools.partial(far_copy, h, 0, every, ob))
+
+        def far_middle(h):
+            if ring:
+                for origin, zs, to in ((3, low, 1), (1, high, 3)):
+                    far_arrival(h, origin, zs, to).wait_recv()
+                    started(last, functools.partial(far_copy, h, origin, zs, to))
+
+        both_parts = range(PARTS)
+        a_start()
+        run(queue, beside[0])
+        for h in both_parts:
+            a_middle(h)
+        run(queue, beside[1])
+        for h in both_parts:
+            a_close(h)
+        run(queue, beside[2])
+        for h in both_parts:
+            b_close(h)
+        run(queue, beside[3])
+        for h in both_parts:
+            z_close(h)
+        run(queue, beside[4])
+        for h in both_parts:
+            near_start(h)
+        run(queue, beside[5])
+        for h in both_parts:
+            far_start(h)
+        run(queue, beside[6])
+        for h in both_parts:
+            far_middle(h)
+        run(queue, len(queue))
+        flush(sent)
+        inverse_here(level + 1)
+        total = jnp.zeros((2 * WIDTH, VECS), jnp.float32)
+
+        def products(total, at):
+            for ox, oy in at:
+                total += product(level + 1, full, *plan[0][2](oy, ox))
+            return total
+
         if ring:
-            for ob in order:
-                slab = slab_at(2, ob)
-                sums[slab] = terms(slab).astype(jnp.bfloat16)
-                start(functools.partial(a_half, 0, ob))
-                start(functools.partial(a_half, 1, ob))
-            for ob in order:
-                for kind, oa in ((0, 1), (1, 3)):
-                    slab = slab_at(oa, ob)
-                    value = terms(slab)
-                    a_half(kind, ob).wait_recv()
-                    zs = (low, high)[kind]
-                    extra = ra[1, ob, zs].astype(jnp.float32)
-                    halves = [value[: NZ // 2], value[NZ // 2 :]]
-                    halves[kind] = halves[kind] + extra
-                    sums[slab] = jnp.concatenate(halves, axis=0).astype(jnp.bfloat16)
-                    start(functools.partial(a_copy, oa, ob))
+            for h in both_parts:
+                far_arrival(h, 3, high, 1).wait_recv()
+                far_arrival(h, 1, low, 3).wait_recv()
+            total = products(total, [(ox, oy) for ox in (0, 1, 3) for oy in (0, 1, 3)])
+            for h in both_parts:
+                far_arrival(h, 2, low, 2).wait_recv()
+                far_arrival(h, 2, high, 2).wait_recv()
+            total = products(total, [(ox, oy) for ox in range(4) for oy in range(4) if 2 in (ox, oy)])
         else:
-            for ob in order:
-                for oa in range(1, na):
-                    slab = slab_at(oa, ob)
-                    sums[slab] = terms(slab).astype(jnp.bfloat16)
-                    start(functools.partial(a_copy, oa, ob))
-        run(queue, beside[0])
-        for ob in order:
-            value = terms(slab_at(0, ob))
-            for oa in (1, 3) if ring else range(1, na):
-                a_copy(oa, ob).wait_recv()
-                value += ra[oa - 1, ob].astype(jnp.float32)
-            if ob:
-                totals[ob] = value.astype(jnp.bfloat16)
-                start(functools.partial(b_copy, ob))
-            else:
-                whole[...] = value
-        run(queue, beside[1])
-        value = whole[...]
-        for ob in range(1, nb):
-            b_copy(ob).wait_recv()
-            value += rb[ob - 1].astype(jnp.float32)
-        whole[...] = value
-        totals[0] = value.astype(jnp.bfloat16)
-        for o in range(1, NZ):
-            start(functools.partial(z_copy, o))
-        run(queue, beside[2])
-        value = whole[z]
-        for o in range(1, NZ):
-            z_copy(o).wait_recv()
-            value += landed[o - 1].astype(jnp.float32)
-        return value
-
-    def of_two(slab, first):
-        blocks = placed_two[pl.ds((first + slab) * NZ, NZ)].reshape(NZ * WIDTH, 2 * WIDTH)
-        return jnp.dot(blocks, solved[0], preferred_element_type=jnp.float32)
-
-    def of_one(slab):
-        blocks = placed_one[pl.ds(slab * NZ, NZ)].reshape(NZ * WIDTH, 2 * WIDTH)
-        return jnp.dot(blocks, solved[1], preferred_element_type=jnp.float32)
-
-    full_two[y, z, c] = rhs_two[...].astype(jnp.bfloat16)
+            for h in both_parts:
+                nb = plan[h][1][0]
+                for ob in range(1, nb):
+                    far_arrival(h, nb - ob, every, ob).wait_recv()
+            total = products(total, [(ox, oy) for ox in range(nx) for oy in range(NY)])
+        conclude(level + 1, total, out, last)
+
+    def of_list(placed, which, first, at, rows):
+        blocks = placed[pl.ds((first + at[0] * NY + at[1]) * NZ, NZ), rows]
+        return jnp.dot(
+            blocks.reshape(-1, 2 * WIDTH), solved[which], preferred_element_type=jnp.float32
+        ).reshape(*blocks.shape[:2], VECS)
+
+    full_two[0, y, z, c] = rhs_two[...].astype(jnp.bfloat16)
     for full in (full_two, full_one, full_root):
         def blank(slab, carry, full=full):
-            full[slab, :, other] = jnp.zeros((NZ, WIDTH, VECS), jnp.bfloat16)
+            full[slab // NY, slab % NY, :, other] = jnp.zeros((NZ, WIDTH, VECS), jnp.bfloat16)
             return carry
 
-        lax.fori_loop(0, full.shape[0], blank, 0)
+        lax.fori_loop(0, full.shape[0] * NY, blank, 0)
     pl.semaphore_wait(barrier, len(greeted))
     root_blocks = placed_one.shape[0]
 
@@ -378,43 +463,21 @@
     def wait_index(which):
         index_copy(which).wait()
 
-    def top(core):
-        sent = []
-        queue = [
-            start_two, lambda: turn(0), lambda: wait_index(0),
-            *fetches(0, root_blocks, placed_two.shape[0], 16),
-        ]
-        gather(core, 0, 1, full_two, sol_two, sent, queue, (1, 4, 2, 1))
-        run(queue, len(queue))
-
     by_core(top)
 
-    def middle(core):
-        sent = []
-        queue = [
-            start_one, lambda: turn(1), lambda: wait_index(1),
-            *fetches(0, 0, root_blocks, 16), *fetches(1, 0, root_blocks, 16),
-        ]
-        moved = reduce(
-            core, 0, 2, lambda slab: of_two(slab, ROOT_SLABS).reshape(NZ, WIDTH, VECS), level_refs["one"], sent, queue,
-            (4, 1, 3),
-        )
-        full_one[pair * NY + y, z, c] = (rhs_one[...] - moved).astype(jnp.bfloat16)
-        gather(core, 1, 2, full_one, sol_one, sent, queue, (3, 2, 1, 1))
-        run(queue, len(queue))
-
-    by_core(middle)
-
-    def bottom(core):
-        sent = []
-        moved = reduce(
-            core, 1, 4, lambda slab: (of_two(slab, 0) + of_one(slab)).reshape(NZ, WIDTH, VECS), level_refs["root"],
-            sent, [], (0, 0, 0),
-        )
-        full_root[x * NY + y, z, c] = (rhs_root[...] - moved).astype(jnp.bfloat16)
-        gather(core, 2, 4, full_root, sol_root, sent, [], (0, 0, 0, 0))
-
-    by_core(bottom)
+    queue = [
+        start_one, lambda: turn(1), *fetches(0, 0, root_blocks, 16), lambda: wait_index(1),
+        *fetches(1, 0, root_blocks, 16),
+    ]
+    level_down(
+        0, 2, lambda at, rows: of_list(placed_two, 0, ROOT_SLABS, at, rows), level_refs["one"],
+        rhs_one, full_one, sol_one, queue, (3, 0, 2, 3, 3, 2, 2),
+    )
+
+    level_down(
+        1, 4, lambda at, rows: of_list(placed_two, 0, 0, at, rows) + of_list(placed_one, 1, 0, at, rows),
+        level_refs["root"], rhs_root, full_root, sol_root, [], (0,) * 7,
+    )
     for which in range(2):
         lower_copy(which).wait_send()
     for level in range(3):
@@ -435,7 +498,7 @@
 
     def level(nx):
         return [
-            planes(nx * NY, NZ), planes(3, NY, NZ), planes(NY, NZ), planes(3, NZ),
+            planes(3, NY, NZ), planes(3, NY, NZ), planes(NY, NZ), planes(3, NZ),
             pltpu.VMEM((NZ, WIDTH, VECS), jnp.float32), planes(NZ - 1),
         ]
 
@@ -459,9 +522,9 @@
             pltpu.VMEM((length + 8, 2 * WIDTH), jnp.float32),
             pltpu.VMEM((blocks_two, WIDTH, 2 * WIDTH), bf16),
             pltpu.VMEM((blocks_one, WIDTH, 2 * WIDTH), bf16),
-            planes(NY, NZ, NC),
-            planes(2 * NY, NZ, NC),
-            planes(NX * NY, NZ, NC),
+            planes(1, NY, NZ, NC),
+            planes(2, NY, NZ, NC),
+            planes(NX, NY, NZ, NC),
             pltpu.VMEM((2, 2 * WIDTH, VECS), bf16),
             pltpu.VMEM((3, 2 * WIDTH, VECS), jnp.float32),
             pltpu.VMEM((3, 2 * WIDTH, VECS), jnp.float32),
@@ -472,12 +535,12 @@
             sems((2, 2)),
             sems((2, 3)),
             sems((2, 3)),
-            sems((2, 3, NZ)),
-            sems((2, 3, 4)),
-            sems((2, 3, 4, 4)),
-            sems((2, 2, NZ)),
-            sems((2, 2, 4, 4)),
-            sems((2, 2, 4)),
+            sems((2, 3, PARTS, NZ)),
+            sems((2, 3, PARTS, 4)),
+            sems((2, 3, PARTS, 4, 2)),
+            sems((2, 2, PARTS, NZ)),
+            sems((2, 2, PARTS, 4, 2)),
+            sems((2, 2, PARTS, 4)),
         ],
         compiler_params=pltpu.CompilerParams(
             collective_id=0, has_side_effects=True, vmem_limit_bytes=60 * 2**20

time: 122 us -> 112 us (0.918)
  Pallas kernels: 121 us -> 111 us
    pallas_call x1, Pallas kernels: 119 us -> 109 us  [substitute(): pl.pallas_call(main_kernel, out_shape=(out, out, out), in_specs=[vmem] *...]
where the time goes in v4:
time: 112 us; the launch traced here: 111 us
  Pallas kernels  111 us (99%)
    pallas_call x1, Pallas kernels, substitute(): pl.pallas_call(main_kernel, out_shape=(out, out, out), in_specs=[vmem] *...  109 us

profile of v4, /device:TPU:1, one launch (start us, length us, event | category | flops | bytes accessed | tf_op | source)
XLA Modules:
  0.0 111.4 jit_solution(13433520712631489915)
XLA Ops:
  0.6 109.4 %shard_map.139 = (f32[64,128]{1,0:T(8,128)}, f32[64,128]{1,0:T(8,128)}, f32[64,128]{1,0:T(8,128)}) custom-call(f32[64,128]{1,0:T(8,128)} %bitcast.6, f32[64,128]{1,0:T(8,128)} %bitcast.7, f32[64,128]{1,0:T(8,128)} %bitcast.8, bf16[64,16384]{1,0:T(8,128)(2,1)} %inv_root_hbm.1, bf16[64,8192]{1,0:T(8,128)(2,1)} %inv_one_hbm.1, bf16[64,4096]{1,0:T(8,128)(2,1)} %inv_two_hbm.1, ...), custom_call_target="tpu_custom_call" | custom-call | tf_op jit(solution)/shard_map/pallas_call | solution.py:507
  110.0 1.4 %shard_map.140 = (f32[64,128]{1,0:T(8,128)}, f32[64,128]{1,0:T(8,128)}, f32[64,128]{1,0:T(8,128)}) custom-call(f32[64,128]{1,0:T(8,128)} %get-tuple-element.9.refs_0_, f32[64,128]{1,0:T(8,128)} %get-tuple-element.10.refs_1_, f32[64,128]{1,0:T(8,128)} %get-tuple-element.11.refs_2_), custom_call_target="tpu_custom_call" | custom-call | tf_op jit(solution)/shard_map/pallas_call | solution.py:558

commit v5 on v4

--- a/solution.py
+++ b/solution.py
@@ -12,7 +12,9 @@
 MESH = pl.DeviceIdType.MESH
 NX, NY, NZ, NC = 4, 4, 8, 2
 ROOT_SLABS = NX * NY
-PARTS = 2
+PARTS = 4
+FAR_FIRST = (4, 3, 5, 2, 6, 1, 7)
+TOP_ROWS = 48
 
 
 def main_kernel(
@@ -91,10 +93,6 @@
 
         return first, second, offsets
 
-    def by_core(body):
-        for core in range(NC):
-            pl.when(c == core)(functools.partial(body, core))
-
     lists = (
         (rows_two, count_two, x, found_two, index_two, source_two, placed_two),
         (rows_one, count_one, half, found_one, index_one, source_one, placed_one),
@@ -175,6 +173,13 @@
         for _ in range(min(count, len(queue))):
             queue.pop(0)()
 
+    def blank(full):
+        def body(slab, carry):
+            full[slab // NY, slab % NY, :, other] = jnp.zeros((NZ, WIDTH, VECS), jnp.bfloat16)
+            return carry
+
+        lax.fori_loop(0, full.shape[0] * NY, body, 0)
+
     def part_of(h):
         return slice(h * WIDTH // PARTS, (h + 1) * WIDTH // PARTS)
 
@@ -207,33 +212,38 @@
         if level < 2:
             solved[level] = total.astype(jnp.bfloat16)
 
-    def top(core):
+    def top():
         sent = []
-
-        def z_copy(o, arrival=False):
+        rows = (slice(0, TOP_ROWS), slice(TOP_ROWS, WIDTH))
+
+        def z_copy(h, o, arrival=False):
             at = (z + NZ - o) % NZ if arrival else z
-            block = full_two.at[0, y, at, c] if core == 0 else full_two.at[0, :, at, c]
-            return remote(block, block, z_sems, (0, 0, o), z_peer((z + o) % NZ))
-
-        def y_copy(o, arrival=False):
+            block = full_two.at[0, slice(None) if h else y, at, c, rows[h]]
+            return remote(block, block, z_sems, (0, h, o), z_peer((z + o) % NZ))
+
+        def y_copy(h, o, arrival=False):
             at = (y + NY - o) % NY if arrival else y
-            block = full_two.at[0, at, :, c] if core == 0 else full_two.at[0, at, z, c]
-            return remote(block, block, a_sems, (0, 0, o), (x * NY + (y + o) % NY, blk))
-
-        near, far = ((z_copy, NZ), (y_copy, NY))[:: 1 if core == 0 else -1]
-        for o in range(1, near[1]):
-            started(sent, functools.partial(near[0], o))
+            block = full_two.at[0, at, z if h else slice(None), c, rows[h]]
+            return remote(block, block, a_sems, (0, h, o), (x * NY + (y + o) % NY, blk))
+
+        along_z = lambda h: [functools.partial(z_copy, h, o) for o in FAR_FIRST]
+        along_y = lambda h: [functools.partial(y_copy, h, o) for o in range(1, NY)]
+        for make in along_y(1) + along_z(0):
+            started(sent, make)
         start_two()
-        for o in range(1, near[1]):
-            near[0](o, True).wait_recv()
-        for o in range(1, far[1]):
-            started(sent, functools.partial(far[0], o))
+        for first, second in ((along_y(1), along_z(1)), (along_z(0), along_y(0))):
+            for make in first:
+                make(True).wait_recv()
+            for make in second:
+                started(sent, make)
+        blank(full_one)
+        blank(full_root)
         turn(0)
         wait_index(0)
         fetch(0, root_blocks, placed_two.shape[0])
         inverse_here(0)
-        for o in range(1, far[1]):
-            far[0](o, True).wait_recv()
+        for make in along_y(0) + along_z(1):
+            make(True).wait_recv()
         total = jnp.zeros((2 * WIDTH, VECS), jnp.float32)
         for at_y in range(NY):
             total += product(0, full_two, 0, at_y)
@@ -242,7 +252,7 @@
     def level_down(level, nx, terms, refs, rhs, full, out, queue, beside):
         sums, ra, totals, rb, whole, landed = refs
         sent, last = [], []
-        plan = [axes_of(h, nx) for h in range(PARTS)]
+        plan = [axes_of(h % 2, nx) for h in range(PARTS)]
         ring = nx == 4
         low, high, every = slice(0, NZ // 2), slice(NZ // 2, NZ), slice(None)
 
@@ -318,7 +328,7 @@
                 value += rb[ob - 1, :, rows].astype(jnp.float32)
             whole[:, rows] = value
             totals[0, :, rows] = value.astype(jnp.bfloat16)
-            for o in range(1, NZ):
+            for o in FAR_FIRST:
                 started(sent, functools.partial(z_copy, o, h))
 
         def z_close(h):
@@ -329,7 +339,7 @@
                 value += landed[o - 1, rows].astype(jnp.float32)
             at_x, at_y = plan[h][2](0, 0)
             full[at_x, at_y, z, c, rows] = (rhs[rows] - value).astype(jnp.bfloat16)
-            for o in range(1, NZ):
+            for o in FAR_FIRST:
                 started(sent, functools.partial(own_copy, o, h))
 
         def own_copy(o, h, arrival=False):
@@ -345,7 +355,7 @@
         def far_copy(h, origin, zs, to):
             (_, b_peer), offsets = plan[h][1:]
             at_x, at_y = offsets(0, origin)
-            line = (at_x, every) if h == 0 else (every, at_y)
+            line = (at_x, every) if h % 2 == 0 else (every, at_y)
             block = full.at[(*line, zs, c, part_of(h))]
             kind = to if origin == 0 else 2
             return remote(
@@ -355,7 +365,7 @@
         def far_arrival(h, ob, zs, by):
             (nb, b_peer), offsets = plan[h][1:]
             at_x, at_y = offsets(0, ob)
-            line = (at_x, every) if h == 0 else (every, at_y)
+            line = (at_x, every) if h % 2 == 0 else (every, at_y)
             block = full.at[(*line, zs, c, part_of(h))]
             return remote(block, block, b_sems, (level + 1, h, by, {low: 0, high: 1, every: 0}[zs]), b_peer(0 if nb < 2 else 1))
 
@@ -438,12 +448,7 @@
         ).reshape(*blocks.shape[:2], VECS)
 
     full_two[0, y, z, c] = rhs_two[...].astype(jnp.bfloat16)
-    for full in (full_two, full_one, full_root):
-        def blank(slab, carry, full=full):
-            full[slab // NY, slab % NY, :, other] = jnp.zeros((NZ, WIDTH, VECS), jnp.bfloat16)
-            return carry
-
-        lax.fori_loop(0, full.shape[0] * NY, blank, 0)
+    blank(full_two)
     pl.semaphore_wait(barrier, len(greeted))
     root_blocks = placed_one.shape[0]
 
@@ -463,7 +468,7 @@
     def wait_index(which):
         index_copy(which).wait()
 
-    by_core(top)
+    top()
 
     queue = [
         start_one, lambda: turn(1), *fetches(0, 0, root_blocks, 16), lambda: wait_index(1),

time: 112 us -> 109 us (0.973)
  Pallas kernels: 111 us -> 108 us
    pallas_call x1, Pallas kernels: 109 us -> 106 us  [substitute(): pl.pallas_call(main_kernel, out_shape=(out, out, out), in_specs=[vmem] *...]
where the time goes in v5:
time: 109 us; the launch traced here: 108 us
  Pallas kernels  108 us (99%)
    pallas_call x1, Pallas kernels, substitute(): pl.pallas_call(main_kernel, out_shape=(out, out, out), in_specs=[vmem] *...  106 us

profile of v5, /device:TPU:1, one launch (start us, length us, event | category | flops | bytes accessed | tf_op | source)
XLA Modules:
  0.0 108.3 jit_solution(17159875408838599895)
XLA Ops:
  0.6 106.2 %shard_map.139 = (f32[64,128]{1,0:T(8,128)}, f32[64,128]{1,0:T(8,128)}, f32[64,128]{1,0:T(8,128)}) custom-call(f32[64,128]{1,0:T(8,128)} %bitcast.6, f32[64,128]{1,0:T(8,128)} %bitcast.7, f32[64,128]{1,0:T(8,128)} %bitcast.8, bf16[64,16384]{1,0:T(8,128)(2,1)} %inv_root_hbm.1, bf16[64,8192]{1,0:T(8,128)(2,1)} %inv_one_hbm.1, bf16[64,4096]{1,0:T(8,128)(2,1)} %inv_two_hbm.1, ...), custom_call_target="tpu_custom_call" | custom-call | tf_op jit(solution)/shard_map/pallas_call | solution.py:512
  106.9 1.4 %shard_map.140 = (f32[64,128]{1,0:T(8,128)}, f32[64,128]{1,0:T(8,128)}, f32[64,128]{1,0:T(8,128)}) custom-call(f32[64,128]{1,0:T(8,128)} %get-tuple-element.9.refs_0_, f32[64,128]{1,0:T(8,128)} %get-tuple-element.10.refs_1_, f32[64,128]{1,0:T(8,128)} %get-tuple-element.11.refs_2_), custom_call_target="tpu_custom_call" | custom-call | tf_op jit(solution)/shard_map/pallas_call | solution.py:563

commit v6 on v5

--- a/solution.py
+++ b/solution.py
@@ -14,6 +14,7 @@
 ROOT_SLABS = NX * NY
 PARTS = 4
 FAR_FIRST = (4, 3, 5, 2, 6, 1, 7)
+RING_ORDER = {2: (1,), 4: (2, 1, 3)}
 TOP_ROWS = 48
 
 
@@ -282,7 +283,7 @@
         def a_start():
             if not ring:
                 for h in range(PARTS):
-                    for oa in range(1, plan[h][0][0]):
+                    for oa in RING_ORDER[plan[h][0][0]]:
                         make(h, oa)
                         started(sent, functools.partial(a_copy, h, oa, every, oa, oa))
                 return
@@ -310,7 +311,7 @@
             for oa in (1, 3) if ring else range(1, na):
                 for zs in (low, high) if ring else (every,):
                     a_copy(h, oa, zs, oa, oa).wait_recv()
-            for ob in [*range(1, nb), 0]:
+            for ob in [*RING_ORDER[nb], 0]:
                 value = terms(offsets(0, ob), rows)
                 for oa in (1, 3) if ring else range(1, na):
                     value += ra[oa - 1, ob, :, rows].astype(jnp.float32)
@@ -372,7 +373,7 @@
         def near_start(h):
             for o in range(1, NZ):
                 own_copy(o, h, True).wait_recv()
-            for oa in range(1, plan[h][0][0]):
+            for oa in RING_ORDER[plan[h][0][0]]:
                 started(sent, functools.partial(near_copy, oa, h))
 
         def far_start(h):
@@ -382,7 +383,7 @@
                 for to, zs in ((1, low), (3, high), (1, high), (3, low)):
                     started(last, functools.partial(far_copy, h, 0, zs, to))
             else:
-                for ob in range(1, plan[h][1][0]):
+                for ob in RING_ORDER[plan[h][1][0]]:
                     started(last, functools.partial(far_copy, h, 0, every, ob))
 
         def far_middle(h):

time: 109 us -> 108 us (level)
  no operation moved by 1% of the time
where the time goes in v6:
time: 108 us; the launch traced here: 107 us
  Pallas kernels  107 us (99%)
    pallas_call x1, Pallas kernels, substitute(): pl.pallas_call(main_kernel, out_shape=(out, out, out), in_specs=[vmem] *...  105 us

profile of v6, /device:TPU:1, one launch (start us, length us, event | category | flops | bytes accessed | tf_op | source)
XLA Modules:
  0.0 107.4 jit_solution(1496916330764257322)
XLA Ops:
  0.6 105.4 %shard_map.139 = (f32[64,128]{1,0:T(8,128)}, f32[64,128]{1,0:T(8,128)}, f32[64,128]{1,0:T(8,128)}) custom-call(f32[64,128]{1,0:T(8,128)} %bitcast.6, f32[64,128]{1,0:T(8,128)} %bitcast.7, f32[64,128]{1,0:T(8,128)} %bitcast.8, bf16[64,16384]{1,0:T(8,128)(2,1)} %inv_root_hbm.1, bf16[64,8192]{1,0:T(8,128)(2,1)} %inv_one_hbm.1, bf16[64,4096]{1,0:T(8,128)(2,1)} %inv_two_hbm.1, ...), custom_call_target="tpu_custom_call" | custom-call | tf_op jit(solution)/shard_map/pallas_call | solution.py:513
  106.0 1.4 %shard_map.140 = (f32[64,128]{1,0:T(8,128)}, f32[64,128]{1,0:T(8,128)}, f32[64,128]{1,0:T(8,128)}) custom-call(f32[64,128]{1,0:T(8,128)} %get-tuple-element.9.refs_0_, f32[64,128]{1,0:T(8,128)} %get-tuple-element.10.refs_1_, f32[64,128]{1,0:T(8,128)} %get-tuple-element.11.refs_2_), custom_call_target="tpu_custom_call" | custom-call | tf_op jit(solution)/shard_map/pallas_call | solution.py:564
